TPU v7x, 512 devices: a whole 4x4x16 slice. The times are simulated.
512 devices in a mesh: samp: 64 (over y, z), feat: 8 (over x, core).
Axes of the slice: x: 4, y: 4, z: 16, core: 2. Of those that a mesh axis runs over, the one named last changes fastest.
Arguments:
- images: bfloat16 [32768, 3072], P('samp'), may hold values from -6 to 6, as said below
- labels: int32 [32768], P('samp'), may hold values from 0 to 999
- filters: bfloat16 [3, 128, 108], P(None, 'feat'), may hold values from -0.625 to 0.625
- biases: float32 [3, 128], P(None, 'feat'), may hold values from -3 to 3
Outputs:
- coefficients: float32 [1536, 1000], P(None, 'feat')
- residual: float32 [32768, 1000], P('samp', 'feat')
Inputs may be any that keep to these rules, and one draw needn't show every extreme that they name: Every pixel intensity of the images lies between -6 and 6.
All inputs are finite; a program needn't handle non-finite values.
Results may differ from a plain program's by a relative error of at most 0.007.
The roundings to bfloat16 on the way count: a program that leaves them out, or rounds other values in their place, can miss the bound.
Values may be sent and summed in bfloat16 or wider, within the bound.
No kernel may reach another device: no remote copies, remote signals or barrier semaphores. Data moves between devices by JAX's collectives and lax.ppermute only.
A program may use at most 128 MiB of HBM per device.

v0:
```python
import jax
import jax.numpy as jnp
from jax import lax
from jax.sharding import PartitionSpec as P

CLS = 1000
BLOCKS = 3


def featurize(pixels, kernels, offsets):
    row_count = pixels.shape[0]
    filter_count = kernels.shape[0]
    pictures = pixels.reshape(row_count, 3, 32, 32)
    weights = kernels.reshape(filter_count, 3, 6, 6)
    response = lax.conv_general_dilated(
        pictures,
        weights,
        (2, 2),
        "VALID",
        dimension_numbers=("NCHW", "OIHW", "NCHW"),
        preferred_element_type=jnp.float32,
    )
    rectified = jnp.maximum(response + offsets[None, :, None, None], 0.0)
    pooled = rectified.reshape(row_count, filter_count, 2, 7, 2, 7).mean(axis=(3, 5))
    return pooled.reshape(row_count, filter_count * 4).astype(jnp.bfloat16)


def block_features(images, kernels, offsets):
    panel = featurize(images, kernels, offsets)
    return (panel, lax.all_gather(panel, "feat", axis=1, tiled=True))


def inner(left, right):
    return lax.dot_general(
        left, right, (((0,), (0,)), ((), ())), preferred_element_type=jnp.float32
    )


def inner_exact(left, right):
    return lax.dot_general(
        left,
        right,
        (((0,), (0,)), ((), ())),
        precision=lax.Precision.HIGHEST,
        preferred_element_type=jnp.float32,
    )


def solve_block(gram, gradient):
    width = gram.shape[0]
    ridge = 0.1 * jnp.trace(gram) / width + 1e-05
    factor = jnp.linalg.cholesky(gram + ridge * jnp.eye(width, dtype=jnp.float32))
    return jax.scipy.linalg.cho_solve((factor, True), gradient)


def per_device(images, labels, filters, biases):
    row_count = images.shape[0]
    total = row_count * lax.axis_size("samp")
    feat_count = lax.axis_size("feat")
    class_share = CLS // feat_count
    first_class = lax.axis_index("feat") * class_share
    columns = first_class + jnp.arange(class_share, dtype=jnp.int32)
    targets = (labels[:, None] == columns[None, :]).astype(jnp.float32)
    results = []
    residual = targets
    for block_index in range(BLOCKS):
        panel, features = block_features(images, filters[block_index], biases[block_index])
        wide = features.astype(jnp.float32)
        partial_gradient = inner_exact(wide, residual)
        partial_gram = inner(features, features)
        summed, gradient_sum = lax.psum((partial_gram, partial_gradient), "samp")
        gram = summed / total
        gradient = gradient_sum * (CLS / total)
        solved = solve_block(gram, gradient)
        results.append(solved)
        residual = (
            residual
            - jnp.dot(
                wide, solved, precision=lax.Precision.HIGHEST, preferred_element_type=jnp.float32
            )
            / CLS
        )
    return (jnp.concatenate(results, axis=0), residual)


def solution(mesh):
    placed = (P("samp", None), P("samp"), P(None, "feat", None), P(None, "feat"))
    return jax.shard_map(
        per_device,
        mesh=mesh,
        in_specs=placed,
        out_specs=(P(None, "feat"), P("samp", "feat")),
        check_vma=False,
    )
```

profile of v0, /device:TPU:1, one launch (start us, length us, event | category | flops | bytes accessed | tf_op | source)
XLA Modules:
  0.0 1301.8 jit_solution(13256271334253305996)
XLA Ops:
  13.6 13.3 %add_maximum_fusion.2 = f32[512,16,14,14]{0,1,3,2:T(8,128)} fusion(f32[16]{0:T(128)S(1)} %get-tuple-element.97, bf16[512,3,32,32]{0,3,2,1:T(8,128)(2,1)} %bitcast.210, bf16[16,3,6,6]{0,3,2,1:T(8,128)(2,1)S(1)} %reshape_squeeze.9), kind=kOutput, calls=%fused_computation.8 | convolution fusion | flops 350027776 | bytes 9571776 | tf_op jit(solution)/shard_map/conv_general_dilated | solution.py:15
  30.4 19.8 %all_gather.9 = bf16[512,512]{0,1:T(8,128)(2,1)S(1)} all-gather(bf16[512,64]{0,1:T(8,128)(2,1)S(1)} %convert_element_type.28), channel_id=1, replica_groups=mesh['samp'=64,'feat'=8] {'feat'}, dimensions={1}, use_global_device_ids=true | all-gather | bytes 589824 | tf_op jit(solution)/shard_map/all_gather | solution.py:30
  53.4 13.3 %add_maximum_fusion.1 = f32[512,16,14,14]{0,1,3,2:T(8,128)} fusion(f32[16]{0:T(128)S(1)} %get-tuple-element.96, bf16[512,3,32,32]{0,3,2,1:T(8,128)(2,1)} %bitcast.211, bf16[16,3,6,6]{0,3,2,1:T(8,128)(2,1)S(1)} %reshape_squeeze.10), kind=kOutput, calls=%fused_computation.7 | convolution fusion | flops 350027776 | bytes 9571776 | tf_op jit(solution)/shard_map/conv_general_dilated | solution.py:15
  70.2 13.7 %all_gather.10 = bf16[512,512]{0,1:T(8,128)(2,1)S(1)} all-gather(bf16[512,64]{0,1:T(8,128)(2,1)S(1)} %convert_element_type.30), channel_id=1, replica_groups=mesh['samp'=64,'feat'=8] {'feat'}, dimensions={1}, use_global_device_ids=true | all-gather | bytes 589824 | tf_op jit(solution)/shard_map/all_gather | solution.py:30
  85.3 231.4 %all-reduce.12.cloned.1.call-done = (f32[512,512]{0,1:T(8,128)}, f32[512,125]{1,0:T(8,128)}) async-done(((f32[512,512]{0,1:T(8,128)}, f32[512,125]{1,0:T(8,128)}), (f32[512,512]{0,1:T(8,128)}, f32[512,125]{1,0:T(8,128)})) %all-reduce.12.cloned.1.call-update) | async-done | bytes 1304592 | tf_op jit(solution)/shard_map/psum | solution.py:71
  322.4 11.7 cholesky.374
  334.1 9.8 custom-call.33
  344.8 11.7 cholesky.393
  356.5 10.0 custom-call.34
  367.1 11.7 cholesky.414
  379.6 9.8 custom-call.35
  390.0 12.1 cholesky.431
  414.6 39.3 %custom-call.36 = f32[4,128,128]{1,2,0:T(8,128)S(1)} custom-call(f32[4,128,128]{2,1,0:T(8,128)S(1)} %get-tuple-element.24), custom_call_target="InvertDiagBlocksLowerTriangular" | custom-call | tf_op jit(solution)/shard_map/jit(_cho_solve)/triangular_solve | solution.py:53
  462.0 13.3 %add_maximum_fusion = f32[512,16,14,14]{0,1,3,2:T(8,128)} fusion(f32[16]{0:T(128)S(1)} %get-tuple-element.98, bf16[512,3,32,32]{0,3,2,1:T(8,128)(2,1)} %bitcast.212, bf16[16,3,6,6]{0,3,2,1:T(8,128)(2,1)S(1)} %reshape_squeeze.11), kind=kOutput, calls=%fused_computation.6 | convolution fusion | flops 350027776 | bytes 9571776 | tf_op jit(solution)/shard_map/conv_general_dilated | solution.py:15
  478.7 24.1 %all_gather.11 = bf16[512,512]{0,1:T(8,128)(2,1)S(1)} all-gather(bf16[512,64]{0,1:T(8,128)(2,1)S(1)} %convert_element_type.33), channel_id=1, replica_groups=mesh['samp'=64,'feat'=8] {'feat'}, dimensions={1}, use_global_device_ids=true | all-gather | bytes 589824 | tf_op jit(solution)/shard_map/all_gather | solution.py:30
  504.4 227.9 %all-reduce.10.cloned.1.call-done = (f32[512,512]{0,1:T(8,128)}, f32[512,125]{1,0:T(8,128)}) async-done(((f32[512,512]{0,1:T(8,128)}, f32[512,125]{1,0:T(8,128)}), (f32[512,512]{0,1:T(8,128)}, f32[512,125]{1,0:T(8,128)})) %all-reduce.10.cloned.1.call-update) | async-done | bytes 1304592 | tf_op jit(solution)/shard_map/psum | solution.py:71
  738.0 11.7 cholesky.446
  749.8 9.8 custom-call.37
  760.3 11.7 cholesky.465
  773.3 10.2 custom-call.38
  784.2 11.7 cholesky.486
  807.1 11.9 cholesky.503
  830.1 39.3 %custom-call.40 = f32[4,128,128]{1,2,0:T(8,128)S(1)} custom-call(f32[4,128,128]{2,1,0:T(8,128)S(1)} %get-tuple-element.25), custom_call_target="InvertDiagBlocksLowerTriangular" | custom-call | tf_op jit(solution)/shard_map/jit(_cho_solve)/triangular_solve | solution.py:53
  877.4 270.4 %all-reduce.8.cloned.1.call-done = (f32[512,512]{0,1:T(8,128)}, f32[512,125]{1,0:T(8,128)}) async-done(((f32[512,512]{0,1:T(8,128)}, f32[512,125]{1,0:T(8,128)}), (f32[512,512]{0,1:T(8,128)}, f32[512,125]{1,0:T(8,128)})) %all-reduce.8.cloned.1.call-update) | async-done | bytes 1304592 | tf_op jit(solution)/shard_map/psum | solution.py:71
  1153.6 11.7 cholesky.518
  1165.5 9.8 custom-call.41
  1176.6 12.1 cholesky.537
  1190.0 9.8 custom-call.42
  1201.4 11.7 cholesky.558
  1213.8 10.0 custom-call.43
  1224.4 11.7 cholesky.575
  1247.4 39.3 %custom-call.44 = f32[4,128,128]{1,2,0:T(8,128)S(1)} custom-call(f32[4,128,128]{2,1,0:T(8,128)S(1)} %get-tuple-element.26), custom_call_target="InvertDiagBlocksLowerTriangular" | custom-call | tf_op jit(solution)/shard_map/jit(_cho_solve)/triangular_solve | solution.py:53
  (216 shorter events, 135.5 us)
Async XLA Ops:
  7.2 309.5 %all-reduce.12.cloned.1.call-start = ((), (), s32[]{:S(2)}) async-start(), calls=%async_computation.2 | async-start | bytes 2621440 | tf_op jit(solution)/shard_map/psum | solution.py:71
  26.9 24.8 %copy-start.9 = (s32[512]{0:T(512)S(1)}, s32[512]{0:T(512)}, u32[]{:S(2)}) copy-start(s32[512]{0:T(512)} %param.8) | copy-start | bytes 6148
  52.9 679.4 %all-reduce.10.cloned.1.call-start = ((), (), s32[]{:S(2)}) async-start(), calls=%async_computation.1 | async-start | bytes 2621440 | tf_op jit(solution)/shard_map/psum | solution.py:71
  457.1 2.6 copy-start
  457.6 2.1 copy-start.4
  458.2 1.5 copy-start.7
  458.9 0.8 copy-start.8
  459.7 0.7 copy-start.2
  461.7 686.1 %all-reduce.8.cloned.1.call-start = ((), (), s32[]{:S(2)}) async-start(), calls=%async_computation | async-start | bytes 2621440 | tf_op jit(solution)/shard_map/psum | solution.py:71
  873.7 276.7 %copy-start.3 = (f32[128,125]{1,0:T(8,128)}, f32[128,125]{1,0:T(8,128)S(1)}, u32[]{:S(2)}) copy-start(f32[128,125]{1,0:T(8,128)S(1)} %fusion.156) | copy-start | bytes 192004
  874.4 276.0 %copy-start.6 = (f32[128,125]{1,0:T(8,128)}, f32[128,125]{1,0:T(8,128)S(1)}, u32[]{:S(2)}) copy-start(f32[128,125]{1,0:T(8,128)S(1)} %fusion.155) | copy-start | bytes 192004
  1165.5 127.7 %copy-start.1 = (f32[128,125]{1,0:T(8,128)S(1)}, f32[128,125]{1,0:T(8,128)}, u32[]{:S(2)}) copy-start(f32[128,125]{1,0:T(8,128)} %copy-done) | copy-start | bytes 192004
  1175.9 0.7 copy-start.5
Sparse Core Ops, SparseCore 0:
  53.0 263.6 all-reduce.11
  461.9 270.3 all-reduce.9
  877.5 270.2 all-reduce.7
where the time goes:
time: 1320 us; the launch traced here: 1300 us
  waiting for transfers between devices  730 us (55%)
  other arithmetic  385 us (29%)
  matrix products  70.1 us (5%)
  blocking collectives  57.6 us (4%)
  local copies, waits for them, and re-layouts  33.8 us (3%)
  between operations  24.4 us (2%)
    psum x3, waiting for transfers between devices, per_device(): summed, gradient_sum = lax.psum((partial_gram, partial_gradient), 'samp')  730 us
    another operation x44, other arithmetic, solve_block(): jnp.linalg.cholesky(gram + ridge * jnp.eye(width, dtype=jnp.float32))  238 us
    another operation x7, other arithmetic, solve_block(): return jax.scipy.linalg.cho_solve((factor, True), gradient)  118 us
    all_gather x3, blocking collectives, block_features(): return (panel, lax.all_gather(panel, 'feat', axis=1, tiled=True))  57.6 us
    conv_general_dilated x3, matrix products, featurize(): lax.conv_general_dilated(pictures, weights, (2, 2), 'VALID', dimension_nu...  40 us
  transfers between devices with their start and end apart: 3, of which 3 were waited for; matrix products, arithmetic and copies ran while one was open for 3% of the time, Pallas kernels for 0%

commit v1 on v0

v1 whole, which is shorter than its diff:
```python
import numpy as np
import jax
import jax.numpy as jnp
from jax import lax
from jax.experimental import pallas as pl
from jax.experimental.pallas import tpu as pltpu
from jax.sharding import Mesh, PartitionSpec as P

CLS = 1000
BLOCKS = 3
BLK = 512
SAMPLES = 32768
ROWS = 512
SHARE = 125
TILE = 128
LOCAL = 48
F32 = jnp.float32
BF16 = jnp.bfloat16
VMEM = pltpu.VMEM
VMEM_LIMIT = 56 << 20

DIAG = [(b, i, j) for b in range(BLOCKS) for i in range(4) for j in range(i + 1)]
CROSS = [(b, a, i, j) for b in range(BLOCKS) for a in range(b) for i in range(4) for j in range(4)]
DIAG_SLOTS, CROSS_SLOTS = 4, 6


def tile_tables():
    table = np.zeros((8, 2 * (DIAG_SLOTS + CROSS_SLOTS)), np.int32)
    for feat in range(8):
        pairs = []
        for slot in range(DIAG_SLOTS):
            b, i, j = DIAG[min(feat * DIAG_SLOTS + slot, len(DIAG) - 1)]
            pairs.append((b * 4 + i, b * 4 + j))
        for slot in range(CROSS_SLOTS):
            b, a, i, j = CROSS[feat * CROSS_SLOTS + slot]
            pairs.append((b * 4 + i, a * 4 + j))
        table[feat] = np.array(pairs, np.int32).reshape(-1)
    return table


def tap_places():
    places = np.zeros((108, 768), np.float32)
    for c in range(3):
        for a in range(6):
            for b in range(6):
                places[c * 36 + a * 6 + b, c * 256 + a * 32 + b] = 1.0
    return places


def full_specs(count):
    return [pl.BlockSpec(memory_space=VMEM)] * count


def dot_nt(left, right):
    return lax.dot_general(left, right, (((1,), (1,)), ((), ())), preferred_element_type=F32)


def dot_exact(left, right):
    return lax.dot_general(
        left, right, (((1,), (0,)), ((), ())), precision=lax.Precision.HIGHEST, preferred_element_type=F32
    )


def conv_kernel(x_ref, w_ref, place_ref, bias_ref, o_ref, taps, acc, mixed):
    base = lax.dot_general(
        w_ref[...], place_ref[...], (((1,), (0,)), ((), ())), preferred_element_type=F32
    )
    for p in range(2):
        for q in range(14):
            shift = 64 * p + 2 * q
            moved = base if shift == 0 else pltpu.roll(base, shift, 1)
            row = (p * 14 + q) * LOCAL
            taps[row : row + LOCAL, :] = moved.astype(BF16)
    acc[...] = jnp.zeros_like(acc)
    bias = jnp.broadcast_to(bias_ref[...], (LOCAL, ROWS))

    def step(t, carry):
        chunks = []
        for c in range(3):
            start = pl.multiple_of(c * 1024 + t * 128, 128)
            chunks.append(x_ref[:, pl.ds(start, 256)])
        pixels = jnp.concatenate(chunks, axis=1)
        for p in range(2):
            top = lax.select(2 * t + p >= 7, 2, 0)
            response = dot_nt(taps[p * 14 * LOCAL : (p + 1) * 14 * LOCAL, :], pixels)
            for j in range(2):
                total = None
                for q in range(7 * j, 7 * j + 7):
                    part = jnp.maximum(response[q * LOCAL : (q + 1) * LOCAL] + bias, 0.0)
                    total = part if total is None else total + part
                acc[top + j] += total
        return carry

    lax.fori_loop(0, 7, step, 0)
    for quadrant in range(4):
        for block in range(ROWS // TILE):
            lanes = slice(block * TILE, (block + 1) * TILE)
            mixed[block, pl.ds(quadrant, LOCAL, stride=4), :] = acc[quadrant, :, lanes] / 49.0
    for block in range(ROWS // TILE):
        o_ref[:, block * TILE : (block + 1) * TILE] = mixed[block].astype(BF16)


def local_features(images, weights, offsets):
    return pl.pallas_call(
        conv_kernel,
        out_shape=jax.ShapeDtypeStruct((4 * LOCAL, ROWS), BF16),
        in_specs=full_specs(4),
        out_specs=pl.BlockSpec(memory_space=VMEM),
        scratch_shapes=[
            VMEM((28 * LOCAL, 768), BF16),
            VMEM((4, LOCAL, ROWS), F32),
            VMEM((ROWS // TILE, 4 * LOCAL, TILE), F32),
        ],
        compiler_params=pltpu.CompilerParams(vmem_limit_bytes=VMEM_LIMIT),
        name="features",
    )(images, weights, jnp.asarray(tap_places(), BF16), offsets)


def products_kernel(feat_ref, table_ref, ft_ref, labels_ref, o_ref):
    feat = feat_ref[0]

    def tile(slot):
        left = pl.multiple_of(table_ref[feat, 2 * slot] * TILE, TILE)
        right = pl.multiple_of(table_ref[feat, 2 * slot + 1] * TILE, TILE)
        return dot_nt(ft_ref[pl.ds(left, TILE), :], ft_ref[pl.ds(right, TILE), :]).reshape(16, 8, TILE)

    for slot in range(DIAG_SLOTS):
        o_ref[16 * slot : 16 * slot + 16, 0:8, :] = tile(slot)
    for slot in range(8):
        unit, place = slot // 4, slot % 4
        value = tile(DIAG_SLOTS + slot) if slot < CROSS_SLOTS else jnp.zeros((16, 8, TILE), F32)
        o_ref[16 * place : 16 * place + 16, 8 + 8 * unit : 16 + 8 * unit, :] = value
    local_class = lax.broadcasted_iota(jnp.int32, (TILE, ROWS), 0)
    hit = (labels_ref[...] == local_class + feat * SHARE) & (local_class < SHARE)
    targets = jnp.where(hit, 1.0, 0.0).astype(BF16)
    for part in range(4):
        rows = slice(part * 384, (part + 1) * 384)
        o_ref[16 * part : 16 * part + 16, 24:48, :] = dot_nt(ft_ref[rows, :], targets).reshape(16, 24, TILE)


def local_products(feat, features, labels):
    return pl.pallas_call(
        products_kernel,
        out_shape=jax.ShapeDtypeStruct((64, 48, TILE), F32),
        in_specs=[pl.BlockSpec(memory_space=pltpu.SMEM)] * 2 + full_specs(2),
        out_specs=pl.BlockSpec(memory_space=VMEM),
        compiler_params=pltpu.CompilerParams(vmem_limit_bytes=VMEM_LIMIT),
        name="products",
    )(feat, jnp.asarray(tile_tables()), features, labels)


def small_inverse(columns, sub):
    for r in range(8):
        row = [jnp.broadcast_to(columns[j][r : r + 1, :], (8, TILE)) for j in range(8)]
        reciprocal = 1.0 / row[r]
        pivot = columns[r]
        following = []
        for j in range(8):
            if j == r:
                following.append(jnp.where(sub == r, reciprocal, -pivot * reciprocal))
            else:
                scaled = row[j] * reciprocal
                following.append(jnp.where(sub == r, scaled, columns[j] - pivot * scaled))
        columns = following
    return columns


def invert_tiles(work):
    count = work.shape[0]
    lane = lax.broadcasted_iota(jnp.int32, (8, TILE), 1)
    sub = lax.broadcasted_iota(jnp.int32, (8, TILE), 0)
    for k in range(16):
        low = 8 * k
        inside = (lane >= low) & (lane < low + 8)
        unit = jnp.where(lane == sub + low, 1.0, 0.0)
        for m in range(count):
            panel = work[m, k]
            columns = [jnp.broadcast_to(panel[:, low + j : low + j + 1], (8, TILE)) for j in range(8)]
            columns = small_inverse(columns, sub)
            source = jnp.where(inside, unit, panel)
            solved = None
            for j in range(8):
                term = columns[j] * jnp.broadcast_to(source[j : j + 1, :], (8, TILE))
                solved = term if solved is None else solved + term
            work[m, k] = solved
            rows = [jnp.broadcast_to(solved[j : j + 1, :], (8, TILE)) for j in range(8)]
            for i in range(16):
                if i == k:
                    continue
                value = work[m, i]
                total = jnp.where(inside, 0.0, value)
                for j in range(8):
                    total = total - jnp.broadcast_to(value[:, low + j : low + j + 1], (8, TILE)) * rows[j]
                work[m, i] = total


def inverse_kernel(core_ref, own_ref, other_ref, o_ref, grid, work):
    core = core_ref[0]
    eye = jnp.where(
        lax.broadcasted_iota(jnp.int32, (TILE, TILE), 0) == lax.broadcasted_iota(jnp.int32, (TILE, TILE), 1),
        1.0,
        0.0,
    )
    traces = [jnp.zeros((1, 1), F32)] * BLOCKS
    for place, (b, i, j) in enumerate(DIAG):
        feat, slot = place // DIAG_SLOTS, place % DIAG_SLOTS
        mine, theirs = own_ref[feat // 2, slot], other_ref[feat // 2, slot]
        tile = jnp.where(core == feat % 2, mine, theirs) * (1.0 / SAMPLES)
        grid[b, i, j] = tile
        if i != j:
            grid[b, j, i] = tile.T
        else:
            diagonal = jnp.sum(tile * eye, axis=1, keepdims=True)
            traces[b] = traces[b] + jnp.sum(diagonal, axis=0, keepdims=True)
    for b in range(BLOCKS):
        ridge = 0.1 * traces[b] / BLK + 1e-05
        for i in range(4):
            grid[b, i, i] += ridge * eye

    def pivot(k, carry):
        for b in range(BLOCKS):
            work[b] = grid[b, k, k].reshape(16, 8, TILE)
        invert_tiles(work)
        for b in range(BLOCKS):
            inverse = work[b].reshape(TILE, TILE)
            others = [lax.rem(k + d, 4) for d in (1, 2, 3)]
            for j in others:
                grid[b, k, j] = dot_exact(inverse, grid[b, k, j])
            for i in others:
                left = grid[b, i, k]
                for j in others:
                    grid[b, i, j] -= dot_exact(left, grid[b, k, j])
                grid[b, i, k] = -dot_exact(left, inverse)
            grid[b, k, k] = inverse
        return carry

    lax.fori_loop(0, 4, pivot, 0)
    for b in range(BLOCKS):
        for i in range(4):
            for j in range(4):
                o_ref[b, i * TILE : (i + 1) * TILE, j * TILE : (j + 1) * TILE] = grid[b, i, j]


def inverses(core, own, other):
    return pl.pallas_call(
        inverse_kernel,
        out_shape=jax.ShapeDtypeStruct((BLOCKS, BLK, BLK), F32),
        in_specs=[pl.BlockSpec(memory_space=pltpu.SMEM)] + full_specs(2),
        out_specs=pl.BlockSpec(memory_space=VMEM),
        scratch_shapes=[VMEM((BLOCKS, 4, 4, TILE, TILE), F32), VMEM((BLOCKS, 16, 8, TILE), F32)],
        compiler_params=pltpu.CompilerParams(vmem_limit_bytes=VMEM_LIMIT),
        cost_estimate=pl.CostEstimate(flops=9_000_000_000, bytes_accessed=100_000_000, transcendentals=0),
        name="inverses",
    )(core, own, other)


def solve_kernel(feat_ref, inverse_ref, cross_ref, fty_ref, ft_ref, labels_ref, coef_ref, res_ref, steps):
    for b in range(BLOCKS):
        gradient = fty_ref[b * BLK : (b + 1) * BLK, :] * (CLS / SAMPLES)
        for i in range(4):
            total = gradient[i * TILE : (i + 1) * TILE]
            for a in range(b):
                for j in range(4):
                    feat, slot = divmod(CROSS.index((b, a, i, j)), CROSS_SLOTS)
                    rows = slice(a * BLK + j * TILE, a * BLK + (j + 1) * TILE)
                    total = total - dot_exact(cross_ref[feat, slot] * (1.0 / SAMPLES), steps[rows, :])
            rows = slice(b * BLK + i * TILE, b * BLK + (i + 1) * TILE)
            steps[rows, :] = total
        rows = slice(b * BLK, (b + 1) * BLK)
        steps[rows, :] = dot_exact(inverse_ref[b], steps[rows, :])
    value = steps[...]
    coef_ref[...] = value[:, :SHARE]
    high = value.astype(BF16)
    rest = value - high.astype(F32)
    middle = rest.astype(BF16)
    low = (rest - middle.astype(F32)).astype(BF16)
    fit = None
    for part in (low, middle, high):
        term = lax.dot_general(ft_ref[...], part, (((0,), (0,)), ((), ())), preferred_element_type=F32)
        fit = term if fit is None else fit + term
    classes = lax.broadcasted_iota(jnp.int32, (ROWS, TILE), 1) + feat_ref[0] * SHARE
    targets = jnp.where(labels_ref[...] == classes, 1.0, 0.0)
    res_ref[...] = (targets - fit / CLS)[:, :SHARE]


def solve(feat, inverse, cross, fty, features, labels):
    return pl.pallas_call(
        solve_kernel,
        out_shape=(
            jax.ShapeDtypeStruct((BLOCKS * BLK, SHARE), F32),
            jax.ShapeDtypeStruct((ROWS, SHARE), F32),
        ),
        in_specs=[pl.BlockSpec(memory_space=pltpu.SMEM)] + full_specs(5),
        out_specs=(pl.BlockSpec(memory_space=VMEM), pl.BlockSpec(memory_space=VMEM)),
        scratch_shapes=[VMEM((BLOCKS * BLK, TILE), F32)],
        compiler_params=pltpu.CompilerParams(vmem_limit_bytes=VMEM_LIMIT),
        name="solve",
    )(feat, inverse, cross, fty, features, labels)


def gather_by_exchange(value, axis, size):
    copies = jnp.broadcast_to(value[None], (size,) + value.shape)
    return lax.all_to_all(copies, axis, 0, 0, tiled=True)


def swap_cores(value):
    return lax.ppermute(value, "c", [(0, 1), (1, 0)])


def per_device(images, labels, filters, biases):
    core = lax.axis_index("c")
    feat = (lax.axis_index("x") * 2 + core).reshape(1)
    core1 = core.reshape(1)
    panel = local_features(images, filters.reshape(LOCAL, 108), biases.reshape(LOCAL, 1))
    own = lax.all_gather(panel, "x", axis=0)
    other = swap_cores(own)
    pair = jnp.where(core == 0, jnp.stack([own, other]), jnp.stack([other, own]))
    features = pair.reshape(2, 4, BLOCKS, 64, ROWS).transpose(2, 1, 0, 3, 4).reshape(BLOCKS * BLK, ROWS)

    pieces = local_products(feat, features, labels.reshape(1, ROWS))
    pieces = lax.all_to_all(pieces.reshape(4, 16 * 48, TILE), "y", 0, 0, tiled=True)
    pieces = jnp.sum(pieces, axis=0).reshape(16, 48, TILE)
    pieces = jnp.sum(lax.all_to_all(pieces, "z", 0, 0, tiled=True), axis=0)
    column = gather_by_exchange(pieces, "z", 16)

    diagonal = lax.all_gather(column[:, :8], "y", axis=0).reshape(DIAG_SLOTS, TILE, TILE)
    diag_own = gather_by_exchange(diagonal, "x", 4)
    diag_other = swap_cores(diag_own)

    rest = lax.all_gather(column[:, 8:], "y", axis=0)
    rest, diag_own, diag_other = lax.optimization_barrier((rest, diag_own, diag_other))
    cross = rest[:, :, :16].reshape(64, 2, 8, TILE).transpose(1, 0, 2, 3).reshape(8, TILE, TILE)
    cross = lax.all_gather(cross[:CROSS_SLOTS], ("x", "c"), axis=0)
    fty = rest[:, :, 16:].reshape(BLOCKS * BLK, TILE)

    inverse = inverses(core1, diag_own, diag_other)
    return solve(feat, inverse, cross, fty, features, labels.reshape(ROWS, 1))


def solution(mesh):
    split = Mesh(mesh.devices.reshape(4, 16, 4, 2), ("y", "z", "x", "c"))
    samp, feat = ("y", "z"), ("x", "c")
    return jax.shard_map(
        per_device,
        mesh=split,
        in_specs=(P(samp, None), P(samp), P(None, feat, None), P(None, feat)),
        out_specs=(P(None, feat), P(samp, feat)),
        check_vma=False,
    )
```

time: 1320 us -> 269 us (0.20); the launches traced: 1300 us -> 269 us
  waiting for transfers between devices: 730 us -> 4.18 us
  other arithmetic: 385 us -> 0.39 us
  Pallas kernels: 0 us -> 104 us
  matrix products: 70.1 us -> 0 us
  blocking collectives: 57.6 us -> 114 us
  local copies, waits for them, and re-layouts: 33.8 us -> 7.72 us
  starting transfers between devices: 0.41 us -> 24.4 us
    psum x3 -> x0, waiting for transfers between devices: 730 us -> none  [per_device(): summed, gradient_sum = lax.psum((partial_gram, partial_gradient), 'samp')]
    another operation x51 -> x0, other arithmetic: 356 us -> none  [the longest x44 238 us: solve_block(): jnp.linalg.cholesky(gram + ridge * jnp.eye(width, dtype=jnp.float32))]
    pallas_call x0 -> x4, Pallas kernels: none -> 104 us  [the longest x1 74.2 us: inverses(): pl.pallas_call(inverse_kernel, out_shape=jax.ShapeDtypeStruct((BLOCKS, BL...]
    all_to_all x0 -> x4, blocking collectives: none -> 92.5 us  [the longest x2 42.2 us: gather_by_exchange(): return lax.all_to_all(copies, axis, 0, 0, tiled=True)]
    conv_general_dilated x3 -> x0, matrix products: 40 us -> none  [featurize(): lax.conv_general_dilated(pictures, weights, (2, 2), 'VALID', dimension_nu...]
    all_gather x3 -> x2, blocking collectives: 57.6 us -> 21.5 us  [the longest x1 11.8 us: per_device(): own = lax.all_gather(panel, 'x', axis=0)]
    another operation x55 -> x0, local copies, waits for them, and re-layouts: 24.4 us -> none  [the longest x40 23.9 us: solve_block(): return jax.scipy.linalg.cho_solve((factor, True), gradient)]
    ppermute x0 -> x2, starting transfers between devices: none -> 24.3 us  [swap_cores(): return lax.ppermute(value, 'c', [(0, 1), (1, 0)])]
  transfers between devices with their start and end apart: 3 -> 4, of which waited for: 3 -> 2; matrix products, arithmetic and copies ran while one was open for 3% -> 1% of each run, Pallas kernels for 0% -> 28%
where the time goes in v1:
time: 269 us
  blocking collectives  114 us (42%)
  Pallas kernels  104 us (39%)
  starting transfers between devices  24.4 us (9%)
  between operations  14.1 us (5%)
  local copies, waits for them, and re-layouts  7.72 us (3%)
  waiting for transfers between devices  4.18 us (2%)
    pallas_call x1, Pallas kernels, inverses(): pl.pallas_call(inverse_kernel, out_shape=jax.ShapeDtypeStruct((BLOCKS, BL...  74.2 us
    all_to_all x2, blocking collectives, gather_by_exchange(): return lax.all_to_all(copies, axis, 0, 0, tiled=True)  42.2 us
    all_to_all x1, blocking collectives, per_device(): pieces = jnp.sum(lax.all_to_all(pieces, 'z', 0, 0, tiled=True), axis=0)  26.3 us
    ppermute x2, starting transfers between devices, swap_cores(): return lax.ppermute(value, 'c', [(0, 1), (1, 0)])  24.3 us
    all_to_all x1, blocking collectives, per_device(): lax.all_to_all(pieces.reshape(4, 16 * 48, TILE), 'y', 0, 0, tiled=True)  24 us
    pallas_call x1, Pallas kernels, solve(): pl.pallas_call(solve_kernel, out_shape=(jax.ShapeDtypeStruct((BLOCKS * BL...  13.8 us
    pallas_call x1, Pallas kernels, local_features(): pl.pallas_call(conv_kernel, out_shape=jax.ShapeDtypeStruct((4 * LOCAL, RO...  12.4 us
    all_gather x1, blocking collectives, per_device(): own = lax.all_gather(panel, 'x', axis=0)  11.8 us
  transfers between devices with their start and end apart: 4, of which 2 were waited for; matrix products, arithmetic and copies ran while one was open for 1% of the time, Pallas kernels for 28%

profile of v1, /device:TPU:1, one launch (start us, length us, event | category | flops | bytes accessed | tf_op | source)
XLA Modules:
  0.0 268.7 jit_solution(1117601791669700149)
XLA Ops:
  7.2 0.0 all-gather.7.cloned.1.call-start
  7.2 1.4 reshape.69.bias_ref
  8.6 12.4 %features.1 = bf16[192,512]{1,0:T(8,128)(2,1)} custom-call(bf16[512,3072]{1,0:T(8,128)(2,1)} %x_ref.1, bf16[48,108]{1,0:T(8,128)(2,1)} %bitcast.35, bf16[108,768]{1,0:T(8,128)(2,1)} %constant.18.clone.place_ref, f32[48,1]{1,0:T(8,128)} %reshape.69.bias_ref), custom_call_target="tpu_custom_call" | custom-call | tf_op jit(solution)/shard_map/features/pallas_call | solution.py:104
  21.0 11.8 %all-gather = bf16[768,512]{1,0:T(8,128)(2,1)S(1)} all-gather(bf16[192,512]{1,0:T(8,128)(2,1)} %features.1), channel_id=2, replica_groups=mesh['y'=4,'z'=16,'x'=4,'c'=2] {'x'}, dimensions={0}, use_global_device_ids=true | all-gather | bytes 983040 | tf_op jit(solution)/shard_map/all_gather | solution.py:315
  32.8 10.5 %collective-permute-start = (bf16[4,192,512]{2,1,0:T(8,128)(2,1)S(1)}, bf16[4,192,512]{2,1,0:T(8,128)(2,1)S(1)}, u32[]{:S(2)}, u32[]{:S(2)}) collective-permute-start(bf16[4,192,512]{2,1,0:T(8,128)(2,1)S(1)} %bitcast.26), channel_id=1, source_target_pairs={{0,1},{1,0},{2,3},{3,2},{4,5},{5,4},{6,7},{7,6},{8,9},{9,8},{10,11... | collective-permute-start | bytes 2359304 | tf_op jit(solution)/shard_map/ppermute | solution.py:307
  43.3 1.9 collective-permute-done
  45.2 0.3 fusion
  45.4 1.3 copy.21
  46.7 3.5 %products.1 = f32[64,48,128]{2,1,0:T(8,128)} custom-call(s32[1]{0:T(128)} %bitcast.feat_ref, s32[8,20]{1,0:T(8,128)} %constant.19.clone.table_ref, bf16[1536,512]{1,0:T(8,128)(2,1)} %bitcast.21, s32[1,512]{1,0:T(1,128)} %bitcast.36), custom_call_target="tpu_custom_call" | custom-call | tf_op jit(solution)/shard_map/products/pallas_call | solution.py:142
  50.2 24.0 %all_to_all.20 = f32[4,768,128]{2,1,0:T(8,128)S(1)} all-to-all(f32[4,768,128]{2,1,0:T(8,128)} %bitcast.23), channel_id=1, replica_groups=mesh['y'=4,'z'=16,'x'=4,'c'=2] {'y'}, dimensions={0} | all-to-all | bytes 3145728 | tf_op jit(solution)/shard_map/all_to_all | solution.py:321
  74.2 0.1 reduce_sum.18
  74.3 26.3 %all_to_all.21 = f32[16,48,128]{2,1,0:T(8,128)S(1)} all-to-all(f32[16,48,128]{2,1,0:T(8,128)S(1)} %bitcast.30), channel_id=1, replica_groups=mesh['y'=4,'z'=16,'x'=4,'c'=2] {'z'}, dimensions={0} | all-to-all | bytes 786432 | tf_op jit(solution)/shard_map/all_to_all | solution.py:323
  100.7 28.5 %all_to_all.22 = f32[16,48,128]{2,1,0:T(8,128)S(1)} all-to-all(f32[16,48,128]{2,1,0:T(8,128)S(1)} %broadcast_in_dim.6), channel_id=1, replica_groups=mesh['y'=4,'z'=16,'x'=4,'c'=2] {'z'}, dimensions={0} | all-to-all | bytes 786432 | tf_op jit(solution)/shard_map/all_to_all | solution.py:303
  129.2 0.7 slice.20
  129.9 0.0 all-gather.7.cloned.1.call-update
  129.9 0.0 all-gather.9.cloned.1.call-start
  130.0 9.7 %all-gather.2 = f32[64,8,128]{2,1,0:T(8,128)S(1)} all-gather(f32[16,8,128]{2,1,0:T(8,128)S(1)} %slice.21), channel_id=4, replica_groups=mesh['y'=4,'z'=16,'x'=4,'c'=2] {'y'}, dimensions={0}, use_global_device_ids=true | all-gather | bytes 327680 | tf_op jit(solution)/shard_map/all_gather | solution.py:326
  139.7 0.1 broadcast_in_dim.15
  139.8 13.7 %all_to_all.23.own_ref = f32[4,4,128,128]{3,2,1,0:T(8,128)S(1)} all-to-all(f32[4,4,128,128]{3,2,1,0:T(8,128)S(1)} %broadcast_in_dim.15), channel_id=1, replica_groups=mesh['y'=4,'z'=16,'x'=4,'c'=2] {'x'}, dimensions={0} | all-to-all | bytes 2097152 | tf_op jit(solution)/shard_map/all_to_all | solution.py:303
  153.5 13.9 %collective-permute-start.1 = (f32[4,4,128,128]{3,2,1,0:T(8,128)S(1)}, f32[4,4,128,128]{3,2,1,0:T(8,128)S(1)}, u32[]{:S(2)}, u32[]{:S(2)}) collective-permute-start(f32[4,4,128,128]{3,2,1,0:T(8,128)S(1)} %all_to_all.23.own_ref), channel_id=1, source_target_pairs={{0,1},{1,0},{2,3},{3,2},{4,5},{5,4},{6,7},{7,6},{8,9},{9,8},{10,11... | collective-permute-start | bytes 3145736 | tf_op jit(solution)/shard_map/ppermute | solution.py:307
  167.4 2.3 collective-permute-done.1.other_ref
  169.6 1.5 slice.17
  171.2 0.8 slice.22
  171.9 0.0 all-gather.9.cloned.1.call-update
  172.0 0.0 copy-done.1
  172.0 0.0 copy-done.3
  172.0 0.0 copy-done.2
  172.0 0.9 copy.23.labels_ref
  172.9 0.0 copy-done
  172.9 1.0 slice.19
  173.8 74.2 %inverses.1.inverse_ref = f32[3,512,512]{2,1,0:T(8,128)} custom-call(s32[1]{0:T(128)} %bitcast.1.core_ref, f32[4,4,128,128]{3,2,1,0:T(8,128)} %copy-done.1, f32[4,4,128,128]{3,2,1,0:T(8,128)} %copy-done.3), custom_call_target="tpu_custom_call" | custom-call | flops 8999999488 | bytes 100000000 | tf_op jit(solution)/shard_map/inverses/pallas_call | solution.py:245
  248.0 13.8 %solve.1 = (f32[1536,125]{1,0:T(8,128)}, f32[512,125]{1,0:T(8,128)}) custom-call(s32[1]{0:T(128)} %bitcast.feat_ref, f32[3,512,512]{2,1,0:T(8,128)} %inverses.1.inverse_ref, f32[8,6,128,128]{3,2,1,0:T(8,128)} %bitcast.25, f32[1536,128]{1,0:T(8,128)} %bitcast.24, bf16[1536,512]{1,0:T(8,128)(2,1)} %bitcast.22, s32[512,1]{1,0:T(8,128)} %copy.23.labels_ref), custom_call_target="tpu_custom_call" | custom-call | tf_op jit(solution)/shard_map/solve/pallas_call | solution.py:287
  (10 shorter events, 0.1 us)
Async XLA Ops:
  7.2 162.5 %all-gather.7.cloned.1.call-start = ((), (), s32[]{:S(2)}) async-start(), calls=%async_computation.4 | async-start | bytes 1638400 | tf_op jit(solution)/shard_map/all_gather | solution.py:330
  32.8 12.4 %collective-permute-start = (bf16[4,192,512]{2,1,0:T(8,128)(2,1)S(1)}, bf16[4,192,512]{2,1,0:T(8,128)(2,1)S(1)}, u32[]{:S(2)}, u32[]{:S(2)}) collective-permute-start(bf16[4,192,512]{2,1,0:T(8,128)(2,1)S(1)} %bitcast.26), channel_id=1, source_target_pairs={{0,1},{1,0},{2,3},{3,2},{4,5},{5,4},{6,7},{7,6},{8,9},{9,8},{10,11... | collective-permute-start | bytes 2359304 | tf_op jit(solution)/shard_map/ppermute | solution.py:307
  129.9 118.1 %all-gather.9.cloned.1.call-start = ((), (), s32[]{:S(2)}) async-start(), calls=%async_computation.5 | async-start | bytes 3538944 | tf_op jit(solution)/shard_map/all_gather | solution.py:333
  153.5 18.5 %copy-start.1 = (f32[4,4,128,128]{3,2,1,0:T(8,128)}, f32[4,4,128,128]{3,2,1,0:T(8,128)S(1)}, u32[]{:S(2)}) copy-start(f32[4,4,128,128]{3,2,1,0:T(8,128)S(1)} %all_to_all.23.own_ref) | copy-start | bytes 3145732
  153.5 16.1 %collective-permute-start.1 = (f32[4,4,128,128]{3,2,1,0:T(8,128)S(1)}, f32[4,4,128,128]{3,2,1,0:T(8,128)S(1)}, u32[]{:S(2)}, u32[]{:S(2)}) collective-permute-start(f32[4,4,128,128]{3,2,1,0:T(8,128)S(1)} %all_to_all.23.own_ref), channel_id=1, source_target_pairs={{0,1},{1,0},{2,3},{3,2},{4,5},{5,4},{6,7},{7,6},{8,9},{9,8},{10,11... | collective-permute-start | bytes 3145736 | tf_op jit(solution)/shard_map/ppermute | solution.py:307
  169.6 2.4 copy-start.3
  169.6 2.4 copy-start.2
  169.6 3.2 %copy-start = (f32[64,40,128]{2,1,0:T(8,128)S(1)}, f32[64,40,128]{2,1,0:T(8,128)}, u32[]{:S(2)}) copy-start(f32[64,40,128]{2,1,0:T(8,128)} %all-gather.7.cloned.1.call-done) | copy-start | bytes 3932164
Sparse Core Ops, SparseCore 0:
  130.1 32.5 all-gather.6
  172.1 30.9 all-gather.8

commit v2 on v1

--- a/solution.py
+++ b/solution.py
@@ -22,6 +22,8 @@
 DIAG = [(b, i, j) for b in range(BLOCKS) for i in range(4) for j in range(i + 1)]
 CROSS = [(b, a, i, j) for b in range(BLOCKS) for a in range(b) for i in range(4) for j in range(4)]
 DIAG_SLOTS, CROSS_SLOTS = 4, 6
+LOWER = [(i, j) for i in range(4) for j in range(i)]
+PANEL = 32
 
 
 def tile_tables():
@@ -55,10 +57,22 @@
     return lax.dot_general(left, right, (((1,), (1,)), ((), ())), preferred_element_type=F32)
 
 
+def exact(left, right, over):
+    return lax.dot_general(
+        left, right, (over, ((), ())), precision=lax.Precision.HIGHEST, preferred_element_type=F32
+    )
+
+
 def dot_exact(left, right):
-    return lax.dot_general(
-        left, right, (((1,), (0,)), ((), ())), precision=lax.Precision.HIGHEST, preferred_element_type=F32
-    )
+    return exact(left, right, ((1,), (0,)))
+
+
+def dot_nt_exact(left, right):
+    return exact(left, right, ((1,), (1,)))
+
+
+def dot_tn_exact(left, right):
+    return exact(left, right, ((0,), (0,)))
 
 
 def conv_kernel(x_ref, w_ref, place_ref, bias_ref, o_ref, taps, acc, mixed):
@@ -72,7 +86,11 @@
             row = (p * 14 + q) * LOCAL
             taps[row : row + LOCAL, :] = moved.astype(BF16)
     acc[...] = jnp.zeros_like(acc)
-    bias = jnp.broadcast_to(bias_ref[...], (LOCAL, ROWS))
+    square = (16, 16)
+    unit = lax.broadcasted_iota(jnp.int32, square, 0) == lax.broadcasted_iota(jnp.int32, square, 1)
+    spread = [jnp.broadcast_to(bias_ref[b : b + 1, :], square) for b in range(BLOCKS)]
+    upright = [jnp.sum(jnp.where(unit, rows, 0.0), axis=1, keepdims=True) for rows in spread]
+    bias = jnp.broadcast_to(jnp.concatenate(upright, axis=0), (LOCAL, ROWS))
 
     def step(t, carry):
         chunks = []
@@ -149,18 +167,36 @@
     )(feat, jnp.asarray(tile_tables()), features, labels)
 
 
-def small_inverse(columns, sub):
+def along_lanes(value, j):
+    return jnp.broadcast_to(value[:, j : j + 1], (8, TILE))
+
+
+def along_rows(value, j):
+    return jnp.broadcast_to(value[j : j + 1, :], (8, TILE))
+
+
+def add_up(terms):
+    while len(terms) > 1:
+        paired = [terms[i] + terms[i + 1] for i in range(0, len(terms) - 1, 2)]
+        terms = paired + ([terms[-1]] if len(terms) % 2 else [])
+    return terms[0]
+
+
+def small_inverses(columns, sub):
+    count = len(columns)
     for r in range(8):
-        row = [jnp.broadcast_to(columns[j][r : r + 1, :], (8, TILE)) for j in range(8)]
-        reciprocal = 1.0 / row[r]
-        pivot = columns[r]
-        following = []
+        here = sub == r
+        rows = [[along_rows(columns[m][j], r) for j in range(8)] for m in range(count)]
+        reciprocals = [1.0 / rows[m][r] for m in range(count)]
+        following = [[None] * 8 for _ in range(count)]
         for j in range(8):
-            if j == r:
-                following.append(jnp.where(sub == r, reciprocal, -pivot * reciprocal))
-            else:
-                scaled = row[j] * reciprocal
-                following.append(jnp.where(sub == r, scaled, columns[j] - pivot * scaled))
+            for m in range(count):
+                pivot = columns[m][r]
+                if j == r:
+                    following[m][j] = jnp.where(here, reciprocals[m], -pivot * reciprocals[m])
+                else:
+                    scaled = rows[m][j] * reciprocals[m]
+                    following[m][j] = jnp.where(here, scaled, columns[m][j] - pivot * scaled)
         columns = following
     return columns
 
@@ -169,32 +205,43 @@
     count = work.shape[0]
     lane = lax.broadcasted_iota(jnp.int32, (8, TILE), 1)
     sub = lax.broadcasted_iota(jnp.int32, (8, TILE), 0)
-    for k in range(16):
-        low = 8 * k
-        inside = (lane >= low) & (lane < low + 8)
-        unit = jnp.where(lane == sub + low, 1.0, 0.0)
+    wide_lane = lax.broadcasted_iota(jnp.int32, (TILE, TILE), 1)
+    for start in range(0, TILE, PANEL):
+        first, steps = start // 8, PANEL // 8
+        whole = [work[m].reshape(TILE, TILE) for m in range(count)]
+        panels = [[work[m, first + i] for i in range(steps)] for m in range(count)]
+        for k in range(steps):
+            low = start + 8 * k
+            inside = (lane >= low) & (lane < low + 8)
+            unit = jnp.where(lane == sub + low, 1.0, 0.0)
+            inverted = small_inverses(
+                [[along_lanes(panels[m][k], low + j) for j in range(8)] for m in range(count)], sub
+            )
+            sources = [jnp.where(inside, unit, panels[m][k]) for m in range(count)]
+            solved = [
+                add_up([inverted[m][j] * along_rows(sources[m], j) for j in range(8)]) for m in range(count)
+            ]
+            rows = [[along_rows(solved[m], j) for j in range(8)] for m in range(count)]
+            following = [[None] * steps for _ in range(count)]
+            for d in range(steps):
+                i = (k + d) % steps
+                for m in range(count):
+                    if d == 0:
+                        following[m][i] = solved[m]
+                        continue
+                    value = panels[m][i]
+                    change = add_up([along_lanes(value, low + j) * rows[m][j] for j in range(8)])
+                    following[m][i] = jnp.where(inside, 0.0, value) - change
+            panels = following
+        inside = (wide_lane >= start) & (wide_lane < start + PANEL)
         for m in range(count):
-            panel = work[m, k]
-            columns = [jnp.broadcast_to(panel[:, low + j : low + j + 1], (8, TILE)) for j in range(8)]
-            columns = small_inverse(columns, sub)
-            source = jnp.where(inside, unit, panel)
-            solved = None
-            for j in range(8):
-                term = columns[j] * jnp.broadcast_to(source[j : j + 1, :], (8, TILE))
-                solved = term if solved is None else solved + term
-            work[m, k] = solved
-            rows = [jnp.broadcast_to(solved[j : j + 1, :], (8, TILE)) for j in range(8)]
-            for i in range(16):
-                if i == k:
-                    continue
-                value = work[m, i]
-                total = jnp.where(inside, 0.0, value)
-                for j in range(8):
-                    total = total - jnp.broadcast_to(value[:, low + j : low + j + 1], (8, TILE)) * rows[j]
-                work[m, i] = total
-
-
-def inverse_kernel(core_ref, own_ref, other_ref, o_ref, grid, work):
+            change = dot_exact(whole[m][:, start : start + PANEL], jnp.concatenate(panels[m], axis=0))
+            work[m] = (jnp.where(inside, 0.0, whole[m]) - change).reshape(16, 8, TILE)
+            for i in range(steps):
+                work[m, first + i] = panels[m][i]
+
+
+def factor_kernel(core_ref, own_ref, other_ref, pivot_ref, lower_ref, grid, work):
     core = core_ref[0]
     eye = jnp.where(
         lax.broadcasted_iota(jnp.int32, (TILE, TILE), 0) == lax.broadcasted_iota(jnp.int32, (TILE, TILE), 1),
@@ -204,12 +251,10 @@
     traces = [jnp.zeros((1, 1), F32)] * BLOCKS
     for place, (b, i, j) in enumerate(DIAG):
         feat, slot = place // DIAG_SLOTS, place % DIAG_SLOTS
-        mine, theirs = own_ref[feat // 2, slot], other_ref[feat // 2, slot]
+        mine, theirs = own_ref[slot, feat // 2], other_ref[slot, feat // 2]
         tile = jnp.where(core == feat % 2, mine, theirs) * (1.0 / SAMPLES)
         grid[b, i, j] = tile
-        if i != j:
-            grid[b, j, i] = tile.T
-        else:
+        if i == j:
             diagonal = jnp.sum(tile * eye, axis=1, keepdims=True)
             traces[b] = traces[b] + jnp.sum(diagonal, axis=0, keepdims=True)
     for b in range(BLOCKS):
@@ -217,85 +262,106 @@
         for i in range(4):
             grid[b, i, i] += ridge * eye
 
-    def pivot(k, carry):
+    for k in range(4):
         for b in range(BLOCKS):
             work[b] = grid[b, k, k].reshape(16, 8, TILE)
         invert_tiles(work)
+        inverse = [work[b].reshape(TILE, TILE) for b in range(BLOCKS)]
+        factors = {}
+        for i in range(k + 1, 4):
+            for b in range(BLOCKS):
+                factors[b, i] = dot_exact(grid[b, i, k], inverse[b])
+            for j in range(k + 1, i + 1):
+                for b in range(BLOCKS):
+                    grid[b, i, j] -= dot_nt_exact(factors[b, i], grid[b, j, k])
         for b in range(BLOCKS):
-            inverse = work[b].reshape(TILE, TILE)
-            others = [lax.rem(k + d, 4) for d in (1, 2, 3)]
-            for j in others:
-                grid[b, k, j] = dot_exact(inverse, grid[b, k, j])
-            for i in others:
-                left = grid[b, i, k]
-                for j in others:
-                    grid[b, i, j] -= dot_exact(left, grid[b, k, j])
-                grid[b, i, k] = -dot_exact(left, inverse)
-            grid[b, k, k] = inverse
-        return carry
-
-    lax.fori_loop(0, 4, pivot, 0)
-    for b in range(BLOCKS):
-        for i in range(4):
-            for j in range(4):
-                o_ref[b, i * TILE : (i + 1) * TILE, j * TILE : (j + 1) * TILE] = grid[b, i, j]
-
-
-def inverses(core, own, other):
+            pivot_ref[b, k] = inverse[b]
+        for i in range(k + 1, 4):
+            for b in range(BLOCKS):
+                for j in range(k):
+                    lower_ref[b, LOWER.index((i, j))] -= dot_exact(factors[b, i], lower_ref[b, LOWER.index((k, j))])
+                lower_ref[b, LOWER.index((i, k))] = -factors[b, i]
+
+
+def factor(core, own, other):
     return pl.pallas_call(
-        inverse_kernel,
-        out_shape=jax.ShapeDtypeStruct((BLOCKS, BLK, BLK), F32),
+        factor_kernel,
+        out_shape=(
+            jax.ShapeDtypeStruct((BLOCKS, 4, TILE, TILE), F32),
+            jax.ShapeDtypeStruct((BLOCKS, len(LOWER), TILE, TILE), F32),
+        ),
         in_specs=[pl.BlockSpec(memory_space=pltpu.SMEM)] + full_specs(2),
-        out_specs=pl.BlockSpec(memory_space=VMEM),
+        out_specs=(pl.BlockSpec(memory_space=VMEM), pl.BlockSpec(memory_space=VMEM)),
         scratch_shapes=[VMEM((BLOCKS, 4, 4, TILE, TILE), F32), VMEM((BLOCKS, 16, 8, TILE), F32)],
         compiler_params=pltpu.CompilerParams(vmem_limit_bytes=VMEM_LIMIT),
         cost_estimate=pl.CostEstimate(flops=9_000_000_000, bytes_accessed=100_000_000, transcendentals=0),
-        name="inverses",
+        name="factor",
     )(core, own, other)
 
 
-def solve_kernel(feat_ref, inverse_ref, cross_ref, fty_ref, ft_ref, labels_ref, coef_ref, res_ref, steps):
+def solve_kernel(feat_ref, pivot_ref, lower_ref, cross_ref, rest_ref, ft_ref, labels_ref, coef_ref, res_ref, steps):
+    fit = jnp.zeros((ROWS, TILE), F32)
     for b in range(BLOCKS):
-        gradient = fty_ref[b * BLK : (b + 1) * BLK, :] * (CLS / SAMPLES)
+        block = slice(b * BLK, (b + 1) * BLK)
+        parts = []
+        gradient = rest_ref[b * 64 // 3 : b * 64 // 3 + 22, 16:40, :].reshape(22 * 24, TILE)
+        gradient = gradient[b * BLK - b * 64 // 3 * 24 :][:BLK] * (CLS / SAMPLES)
         for i in range(4):
             total = gradient[i * TILE : (i + 1) * TILE]
             for a in range(b):
+                tiles = []
                 for j in range(4):
                     feat, slot = divmod(CROSS.index((b, a, i, j)), CROSS_SLOTS)
-                    rows = slice(a * BLK + j * TILE, a * BLK + (j + 1) * TILE)
-                    total = total - dot_exact(cross_ref[feat, slot] * (1.0 / SAMPLES), steps[rows, :])
-            rows = slice(b * BLK + i * TILE, b * BLK + (i + 1) * TILE)
-            steps[rows, :] = total
-        rows = slice(b * BLK, (b + 1) * BLK)
-        steps[rows, :] = dot_exact(inverse_ref[b], steps[rows, :])
-    value = steps[...]
-    coef_ref[...] = value[:, :SHARE]
-    high = value.astype(BF16)
-    rest = value - high.astype(F32)
-    middle = rest.astype(BF16)
-    low = (rest - middle.astype(F32)).astype(BF16)
-    fit = None
-    for part in (low, middle, high):
-        term = lax.dot_general(ft_ref[...], part, (((0,), (0,)), ((), ())), preferred_element_type=F32)
-        fit = term if fit is None else fit + term
-    classes = lax.broadcasted_iota(jnp.int32, (ROWS, TILE), 1) + feat_ref[0] * SHARE
-    targets = jnp.where(labels_ref[...] == classes, 1.0, 0.0)
+                    tiles.append(cross_ref[feat, slot])
+                strip = jnp.concatenate(tiles, axis=1) * (1.0 / SAMPLES)
+                total = total - dot_exact(strip, steps[a * BLK : (a + 1) * BLK, :])
+            parts.append(total)
+        forward = []
+        for i in range(4):
+            total = parts[i]
+            if i:
+                strip = jnp.concatenate([lower_ref[b, LOWER.index((i, j))] for j in range(i)], axis=1)
+                total = total + dot_exact(strip, jnp.concatenate(parts[:i], axis=0))
+            forward.append(dot_exact(pivot_ref[b, i], total))
+        for i in range(4):
+            total = forward[i]
+            if i < 3:
+                strip = jnp.concatenate([lower_ref[b, LOWER.index((j, i))] for j in range(i + 1, 4)], axis=0)
+                total = total + dot_tn_exact(strip, jnp.concatenate(forward[i + 1 :], axis=0))
+            steps[b * BLK + i * TILE : b * BLK + (i + 1) * TILE, :] = total
+        value = steps[block, :]
+        coef_ref[block, :] = value[:, :SHARE]
+        high = value.astype(BF16)
+        left = value - high.astype(F32)
+        middle = left.astype(BF16)
+        low = (left - middle.astype(F32)).astype(BF16)
+        terms = lax.dot_general(
+            ft_ref[block, :],
+            jnp.concatenate([high, middle, low], axis=1),
+            (((0,), (0,)), ((), ())),
+            preferred_element_type=F32,
+        )
+        fit = fit + ((terms[:, 2 * TILE :] + terms[:, TILE : 2 * TILE]) + terms[:, :TILE])
+    local = (labels_ref[...] - feat_ref[0] * SHARE).astype(F32)
+    upright = jnp.broadcast_to(local, (TILE, ROWS)).T
+    classes = lax.broadcasted_iota(jnp.int32, (ROWS, TILE), 1).astype(F32)
+    targets = jnp.where(upright == classes, 1.0, 0.0)
     res_ref[...] = (targets - fit / CLS)[:, :SHARE]
 
 
-def solve(feat, inverse, cross, fty, features, labels):
+def solve(feat, pivots, lower, cross, rest, features, labels):
     return pl.pallas_call(
         solve_kernel,
         out_shape=(
             jax.ShapeDtypeStruct((BLOCKS * BLK, SHARE), F32),
             jax.ShapeDtypeStruct((ROWS, SHARE), F32),
         ),
-        in_specs=[pl.BlockSpec(memory_space=pltpu.SMEM)] + full_specs(5),
+        in_specs=[pl.BlockSpec(memory_space=pltpu.SMEM)] + full_specs(6),
         out_specs=(pl.BlockSpec(memory_space=VMEM), pl.BlockSpec(memory_space=VMEM)),
         scratch_shapes=[VMEM((BLOCKS * BLK, TILE), F32)],
         compiler_params=pltpu.CompilerParams(vmem_limit_bytes=VMEM_LIMIT),
         name="solve",
-    )(feat, inverse, cross, fty, features, labels)
+    )(feat, pivots, lower, cross, rest, features, labels)
 
 
 def gather_by_exchange(value, axis, size):
@@ -311,7 +377,7 @@
     core = lax.axis_index("c")
     feat = (lax.axis_index("x") * 2 + core).reshape(1)
     core1 = core.reshape(1)
-    panel = local_features(images, filters.reshape(LOCAL, 108), biases.reshape(LOCAL, 1))
+    panel = local_features(images, filters.reshape(LOCAL, 108), biases)
     own = lax.all_gather(panel, "x", axis=0)
     other = swap_cores(own)
     pair = jnp.where(core == 0, jnp.stack([own, other]), jnp.stack([other, own]))
@@ -323,18 +389,17 @@
     pieces = jnp.sum(lax.all_to_all(pieces, "z", 0, 0, tiled=True), axis=0)
     column = gather_by_exchange(pieces, "z", 16)
 
-    diagonal = lax.all_gather(column[:, :8], "y", axis=0).reshape(DIAG_SLOTS, TILE, TILE)
-    diag_own = gather_by_exchange(diagonal, "x", 4)
+    diag_own = gather_by_exchange(column[:, :8], ("y", "x"), 16).reshape(DIAG_SLOTS, 4, TILE, TILE)
     diag_other = swap_cores(diag_own)
 
     rest = lax.all_gather(column[:, 8:], "y", axis=0)
     rest, diag_own, diag_other = lax.optimization_barrier((rest, diag_own, diag_other))
-    cross = rest[:, :, :16].reshape(64, 2, 8, TILE).transpose(1, 0, 2, 3).reshape(8, TILE, TILE)
-    cross = lax.all_gather(cross[:CROSS_SLOTS], ("x", "c"), axis=0)
-    fty = rest[:, :, 16:].reshape(BLOCKS * BLK, TILE)
-
-    inverse = inverses(core1, diag_own, diag_other)
-    return solve(feat, inverse, cross, fty, features, labels.reshape(ROWS, 1))
+    rest = rest.reshape(64, 40, TILE)
+    cross = jnp.concatenate([rest[:, 0:8], rest[:32, 8:16]], axis=0).reshape(CROSS_SLOTS, TILE, TILE)
+    cross = lax.all_gather(cross, ("x", "c"), axis=0)
+
+    pivots, lower = factor(core1, diag_own, diag_other)
+    return solve(feat, pivots, lower, cross, rest, features, labels.reshape(1, ROWS))
 
 
 def solution(mesh):

time: 269 us -> 232 us (0.86)
  Pallas kernels: 104 us -> 57.7 us
  waiting for transfers between devices: 4.18 us -> 36.1 us
  blocking collectives: 114 us -> 90.6 us
    pallas_call x1, Pallas kernels: 74.2 us -> 29.7 us  [factor(): pl.pallas_call(factor_kernel, out_shape=(jax.ShapeDtypeStruct((BLOCKS, 4,...]
    all_to_all x2 -> x1, blocking collectives: 42.2 us -> 27.3 us  [gather_by_exchange(): return lax.all_to_all(copies, axis, 0, 0, tiled=True)]
    all_gather x1, waiting for transfers between devices: 0.01 us -> 14.8 us  [per_device(): rest = lax.all_gather(column[:, 8:], 'y', axis=0)]
    all_to_all x0 -> x1, waiting for transfers between devices: none -> 11.3 us  [gather_by_exchange(): return lax.all_to_all(copies, axis, 0, 0, tiled=True)]
    all_gather x1 -> x0, blocking collectives: 9.67 us -> none  [per_device(): lax.all_gather(column[:, :8], 'y', axis=0).reshape(DIAG_SLOTS, TILE, TILE)]
    all_gather x1, waiting for transfers between devices: 0.01 us -> 8.07 us  [per_device(): cross = lax.all_gather(cross, ('x', 'c'), axis=0)]
    all_to_all x0 -> x1, starting transfers between devices: none -> 4.91 us  [gather_by_exchange(): return lax.all_to_all(copies, axis, 0, 0, tiled=True)]
  transfers between devices with their start and end apart: 4 -> 5, of which waited for: 2 -> 4; matrix products, arithmetic and copies ran while one was open for 1% -> 0% of each run, Pallas kernels for 28% -> 13%
where the time goes in v2:
time: 232 us
  blocking collectives  90.6 us (39%)
  Pallas kernels  57.7 us (25%)
  waiting for transfers between devices  36.1 us (16%)
  starting transfers between devices  26.9 us (12%)
  between operations  14.1 us (6%)
  local copies, waits for them, and re-layouts  5.17 us (2%)
    pallas_call x1, Pallas kernels, factor(): pl.pallas_call(factor_kernel, out_shape=(jax.ShapeDtypeStruct((BLOCKS, 4,...  29.7 us
    all_to_all x1, blocking collectives, per_device(): pieces = jnp.sum(lax.all_to_all(pieces, 'z', 0, 0, tiled=True), axis=0)  27.4 us
    all_to_all x1, blocking collectives, gather_by_exchange(): return lax.all_to_all(copies, axis, 0, 0, tiled=True)  27.3 us
    all_to_all x1, blocking collectives, per_device(): lax.all_to_all(pieces.reshape(4, 16 * 48, TILE), 'y', 0, 0, tiled=True)  24 us
    ppermute x2, starting transfers between devices, swap_cores(): return lax.ppermute(value, 'c', [(0, 1), (1, 0)])  21.9 us
    all_gather x1, waiting for transfers between devices, per_device(): rest = lax.all_gather(column[:, 8:], 'y', axis=0)  14.8 us
    pallas_call x1, Pallas kernels, local_features(): pl.pallas_call(conv_kernel, out_shape=jax.ShapeDtypeStruct((4 * LOCAL, RO...  12.5 us
    pallas_call x1, Pallas kernels, solve(): pl.pallas_call(solve_kernel, out_shape=(jax.ShapeDtypeStruct((BLOCKS * BL...  12 us
  transfers between devices with their start and end apart: 5, of which 4 were waited for; matrix products, arithmetic and copies ran while one was open for 0% of the time, Pallas kernels for 13%

profile of v2, /device:TPU:1, one launch (start us, length us, event | category | flops | bytes accessed | tf_op | source)
XLA Modules:
  0.0 231.7 jit_solution(11175348863488350080)
XLA Ops:
  7.2 12.5 %features.1 = bf16[192,512]{1,0:T(8,128)(2,1)} custom-call(bf16[512,3072]{1,0:T(8,128)(2,1)} %x_ref.1, bf16[48,108]{1,0:T(8,128)(2,1)} %bitcast.26, bf16[108,768]{1,0:T(8,128)(2,1)} %constant.18.clone.place_ref, f32[3,16]{1,0:T(4,128)} %bias_ref.1), custom_call_target="tpu_custom_call" | custom-call | tf_op jit(solution)/shard_map/features/pallas_call | solution.py:122
  19.6 11.8 %all-gather = bf16[768,512]{1,0:T(8,128)(2,1)S(1)} all-gather(bf16[192,512]{1,0:T(8,128)(2,1)} %features.1), channel_id=2, replica_groups=mesh['y'=4,'z'=16,'x'=4,'c'=2] {'x'}, dimensions={0}, use_global_device_ids=true | all-gather | bytes 983040 | tf_op jit(solution)/shard_map/all_gather | solution.py:381
  31.4 10.5 %collective-permute-start = (bf16[4,192,512]{2,1,0:T(8,128)(2,1)S(1)}, bf16[4,192,512]{2,1,0:T(8,128)(2,1)S(1)}, u32[]{:S(2)}, u32[]{:S(2)}) collective-permute-start(bf16[4,192,512]{2,1,0:T(8,128)(2,1)S(1)} %bitcast.19), channel_id=1, source_target_pairs={{0,1},{1,0},{2,3},{3,2},{4,5},{5,4},{6,7},{7,6},{8,9},{9,8},{10,11... | collective-permute-start | bytes 2359304 | tf_op jit(solution)/shard_map/ppermute | solution.py:373
  41.9 1.9 collective-permute-done
  43.8 0.3 fusion
  44.1 1.3 copy.12
  45.4 3.5 %products.1 = f32[64,48,128]{2,1,0:T(8,128)} custom-call(s32[1]{0:T(128)} %bitcast.feat_ref, s32[8,20]{1,0:T(8,128)} %constant.19.clone.table_ref, bf16[1536,512]{1,0:T(8,128)(2,1)} %bitcast.16, s32[1,512]{1,0:T(1,128)} %bitcast.27), custom_call_target="tpu_custom_call" | custom-call | tf_op jit(solution)/shard_map/products/pallas_call | solution.py:160
  48.9 24.0 %all_to_all.20 = f32[4,768,128]{2,1,0:T(8,128)S(1)} all-to-all(f32[4,768,128]{2,1,0:T(8,128)} %bitcast.18), channel_id=1, replica_groups=mesh['y'=4,'z'=16,'x'=4,'c'=2] {'y'}, dimensions={0} | all-to-all | bytes 3145728 | tf_op jit(solution)/shard_map/all_to_all | solution.py:387
  72.8 0.1 reduce_sum.18
  73.0 27.4 %all_to_all.21 = f32[16,48,128]{2,1,0:T(8,128)S(1)} all-to-all(f32[16,48,128]{2,1,0:T(8,128)S(1)} %bitcast.22), channel_id=1, replica_groups=mesh['y'=4,'z'=16,'x'=4,'c'=2] {'z'}, dimensions={0} | all-to-all | bytes 786432 | tf_op jit(solution)/shard_map/all_to_all | solution.py:389
  100.5 27.3 %all_to_all.22 = f32[16,48,128]{2,1,0:T(8,128)S(1)} all-to-all(f32[16,48,128]{2,1,0:T(8,128)S(1)} %broadcast_in_dim.4), channel_id=1, replica_groups=mesh['y'=4,'z'=16,'x'=4,'c'=2] {'z'}, dimensions={0} | all-to-all | bytes 786432 | tf_op jit(solution)/shard_map/all_to_all | solution.py:369
  127.8 1.1 broadcast_in_dim.5
  128.9 4.9 %all-to-all-start.3 = ((f32[16,16,8,128]{3,2,1,0:T(8,128)}), f32[16,16,8,128]{3,2,1,0:T(8,128)S(1)}, u32[]{:S(2)}, u32[]{:S(2)}) async-start(f32[16,16,8,128]{3,2,1,0:T(8,128)} %broadcast_in_dim.5), calls=%async_computation.3 | async-start | bytes 2097152 | tf_op jit(solution)/shard_map/all_to_all | solution.py:369
  133.8 0.0 all-gather.7.cloned.1.call-start
  133.8 0.7 slice.16
  134.6 0.0 all-gather.7.cloned.1.call-update
  134.6 0.0 all-gather.5.cloned.1.call-start
  134.7 11.3 %all-to-all-done.3 = f32[16,16,8,128]{3,2,1,0:T(8,128)S(1)} async-done(((f32[16,16,8,128]{3,2,1,0:T(8,128)}), f32[16,16,8,128]{3,2,1,0:T(8,128)S(1)}, u32[]{:S(2)}, u32[]{:S(2)}) %all-to-all-start.3) | async-done | bytes 1048608 | tf_op jit(solution)/shard_map/all_to_all | solution.py:369
  146.0 0.0 copy-start
  146.0 11.4 %collective-permute-start.1 = (f32[4,4,128,128]{3,2,1,0:T(8,128)S(1)}, f32[4,4,128,128]{3,2,1,0:T(8,128)S(1)}, u32[]{:S(2)}, u32[]{:S(2)}) collective-permute-start(f32[4,4,128,128]{3,2,1,0:T(8,128)S(1)} %bitcast.23), channel_id=1, source_target_pairs={{0,1},{1,0},{2,3},{3,2},{4,5},{5,4},{6,7},{7,6},{8,9},{9,8},{10,11... | collective-permute-start | bytes 3145736 | tf_op jit(solution)/shard_map/ppermute | solution.py:373
  157.4 14.8 %all-gather.7.cloned.1.call-done = f32[64,40,128]{2,1,0:T(8,128)} async-done(((f32[16,40,128]{2,1,0:T(8,128)}), f32[64,40,128]{2,1,0:T(8,128)}) %all-gather.7.cloned.1.call-update) | async-done | bytes 1310736 | tf_op jit(solution)/shard_map/all_gather | solution.py:395
  172.3 0.0 collective-permute-done.1.other_ref
  172.3 0.0 copy-start.1
  172.3 1.0 slice.19
  173.3 1.0 slice.18
  174.3 0.8 pad_maximum_fusion
  175.1 0.0 all-gather.5.cloned.1.call-update
  175.1 0.0 copy-done
  175.1 0.0 copy-done.1
  175.1 29.7 %factor.1 = (f32[3,4,128,128]{3,2,1,0:T(8,128)}, f32[3,6,128,128]{3,2,1,0:T(8,128)}) custom-call(s32[1]{0:T(128)} %bitcast.1.core_ref, f32[4,4,128,128]{3,2,1,0:T(8,128)} %bitcast.24, f32[4,4,128,128]{3,2,1,0:T(8,128)} %copy-done.1), custom_call_target="tpu_custom_call" | custom-call | flops 8999999488 | bytes 100000000 | tf_op jit(solution)/shard_map/factor/pallas_call | solution.py:287
  204.8 8.1 %all-gather.5.cloned.1.call-done.cross_ref = f32[8,6,128,128]{3,2,1,0:T(8,128)} async-done(((f32[1,6,128,128]{3,2,1,0:T(8,128)}), f32[8,6,128,128]{3,2,1,0:T(8,128)}) %all-gather.5.cloned.1.call-update) | async-done | bytes 3145744 | tf_op jit(solution)/shard_map/all_gather | solution.py:399
  212.9 12.0 %solve.1 = (f32[1536,125]{1,0:T(8,128)}, f32[512,125]{1,0:T(8,128)}) custom-call(s32[1]{0:T(128)} %bitcast.feat_ref, f32[3,4,128,128]{3,2,1,0:T(8,128)} %get-tuple-element.9.pivot_ref, f32[3,6,128,128]{3,2,1,0:T(8,128)} %get-tuple-element.10.lower_ref, f32[8,6,128,128]{3,2,1,0:T(8,128)} %all-gather.5.cloned.1.call-done.cross_ref, ...), custom_call_target="tpu_custom_call" | custom-call | tf_op jit(solution)/shard_map/solve/pallas_call | solution.py:353
  (3 shorter events, 0.1 us)
Async XLA Ops:
  31.4 12.4 %collective-permute-start = (bf16[4,192,512]{2,1,0:T(8,128)(2,1)S(1)}, bf16[4,192,512]{2,1,0:T(8,128)(2,1)S(1)}, u32[]{:S(2)}, u32[]{:S(2)}) collective-permute-start(bf16[4,192,512]{2,1,0:T(8,128)(2,1)S(1)} %bitcast.19), channel_id=1, source_target_pairs={{0,1},{1,0},{2,3},{3,2},{4,5},{5,4},{6,7},{7,6},{8,9},{9,8},{10,11... | collective-permute-start | bytes 2359304 | tf_op jit(solution)/shard_map/ppermute | solution.py:373
  128.9 17.1 %all-to-all-start.3 = ((f32[16,16,8,128]{3,2,1,0:T(8,128)}), f32[16,16,8,128]{3,2,1,0:T(8,128)S(1)}, u32[]{:S(2)}, u32[]{:S(2)}) async-start(f32[16,16,8,128]{3,2,1,0:T(8,128)} %broadcast_in_dim.5), calls=%async_computation.3 | async-start | bytes 2097152 | tf_op jit(solution)/shard_map/all_to_all | solution.py:369
  133.8 38.5 %all-gather.7.cloned.1.call-start = ((), (), s32[]{:S(2)}) async-start(), calls=%async_computation.5 | async-start | bytes 1638400 | tf_op jit(solution)/shard_map/all_gather | solution.py:395
  134.6 78.3 %all-gather.5.cloned.1.call-start = ((), (), s32[]{:S(2)}) async-start(), calls=%async_computation.4 | async-start | bytes 3538944 | tf_op jit(solution)/shard_map/all_gather | solution.py:399
  146.0 29.1 %copy-start = (f32[16,16,8,128]{3,2,1,0:T(8,128)}, f32[16,16,8,128]{3,2,1,0:T(8,128)S(1)}, u32[]{:S(2)}) copy-start(f32[16,16,8,128]{3,2,1,0:T(8,128)S(1)} %all-to-all-done.3) | copy-start | bytes 3145732
  146.0 26.3 %collective-permute-start.1 = (f32[4,4,128,128]{3,2,1,0:T(8,128)S(1)}, f32[4,4,128,128]{3,2,1,0:T(8,128)S(1)}, u32[]{:S(2)}, u32[]{:S(2)}) collective-permute-start(f32[4,4,128,128]{3,2,1,0:T(8,128)S(1)} %bitcast.23), channel_id=1, source_target_pairs={{0,1},{1,0},{2,3},{3,2},{4,5},{5,4},{6,7},{7,6},{8,9},{9,8},{10,11... | collective-permute-start | bytes 3145736 | tf_op jit(solution)/shard_map/ppermute | solution.py:373
  172.3 2.8 %copy-start.1 = (f32[4,4,128,128]{3,2,1,0:T(8,128)}, f32[4,4,128,128]{3,2,1,0:T(8,128)S(1)}, u32[]{:S(2)}) copy-start(f32[4,4,128,128]{3,2,1,0:T(8,128)S(1)} %collective-permute-done.1.other_ref) | copy-start | bytes 3145732
Sparse Core Ops, SparseCore 0:
  137.3 34.9 all-gather.6
  175.2 37.6 all-gather.4

commit v3 on v2

--- a/solution.py
+++ b/solution.py
@@ -241,7 +241,7 @@
                 work[m, first + i] = panels[m][i]
 
 
-def factor_kernel(core_ref, own_ref, other_ref, pivot_ref, lower_ref, grid, work):
+def factor_kernel(core_ref, own_ref, other_ref, pivot_ref, lower_ref, last_ref, grid, work):
     core = core_ref[0]
     eye = jnp.where(
         lax.broadcasted_iota(jnp.int32, (TILE, TILE), 0) == lax.broadcasted_iota(jnp.int32, (TILE, TILE), 1),
@@ -262,7 +262,7 @@
         for i in range(4):
             grid[b, i, i] += ridge * eye
 
-    for k in range(4):
+    for k in range(3):
         for b in range(BLOCKS):
             work[b] = grid[b, k, k].reshape(16, 8, TILE)
         invert_tiles(work)
@@ -281,30 +281,55 @@
                 for j in range(k):
                     lower_ref[b, LOWER.index((i, j))] -= dot_exact(factors[b, i], lower_ref[b, LOWER.index((k, j))])
                 lower_ref[b, LOWER.index((i, k))] = -factors[b, i]
+    for b in range(BLOCKS):
+        last_ref[b] = grid[b, 3, 3].reshape(16, 8, TILE)
+
+
+def last_kernel(last_ref, o_ref, work):
+    work[...] = last_ref[...]
+    invert_tiles(work)
+    o_ref[...] = work[...].reshape(BLOCKS, TILE, TILE)
+
+
+def last_pivots(last):
+    return pl.pallas_call(
+        last_kernel,
+        out_shape=jax.ShapeDtypeStruct((BLOCKS, TILE, TILE), F32),
+        in_specs=full_specs(1),
+        out_specs=pl.BlockSpec(memory_space=VMEM),
+        scratch_shapes=[VMEM((BLOCKS, 16, 8, TILE), F32)],
+        compiler_params=pltpu.CompilerParams(vmem_limit_bytes=VMEM_LIMIT),
+        cost_estimate=pl.CostEstimate(flops=5_000_000_000, bytes_accessed=10_000_000, transcendentals=0),
+        name="last_pivots",
+    )(last)
 
 
 def factor(core, own, other):
     return pl.pallas_call(
         factor_kernel,
         out_shape=(
-            jax.ShapeDtypeStruct((BLOCKS, 4, TILE, TILE), F32),
+            jax.ShapeDtypeStruct((BLOCKS, 3, TILE, TILE), F32),
             jax.ShapeDtypeStruct((BLOCKS, len(LOWER), TILE, TILE), F32),
+            jax.ShapeDtypeStruct((BLOCKS, 16, 8, TILE), F32),
         ),
         in_specs=[pl.BlockSpec(memory_space=pltpu.SMEM)] + full_specs(2),
-        out_specs=(pl.BlockSpec(memory_space=VMEM), pl.BlockSpec(memory_space=VMEM)),
+        out_specs=(pl.BlockSpec(memory_space=VMEM),) * 3,
         scratch_shapes=[VMEM((BLOCKS, 4, 4, TILE, TILE), F32), VMEM((BLOCKS, 16, 8, TILE), F32)],
         compiler_params=pltpu.CompilerParams(vmem_limit_bytes=VMEM_LIMIT),
-        cost_estimate=pl.CostEstimate(flops=9_000_000_000, bytes_accessed=100_000_000, transcendentals=0),
+        cost_estimate=pl.CostEstimate(flops=25_000_000_000, bytes_accessed=50_000_000, transcendentals=0),
         name="factor",
     )(core, own, other)
 
 
-def solve_kernel(feat_ref, pivot_ref, lower_ref, cross_ref, rest_ref, ft_ref, labels_ref, coef_ref, res_ref, steps):
+def solve_kernel(
+    feat_ref, pivot_ref, last_ref, lower_ref, own_ref, other_ref, rest_ref, ft_ref, labels_ref, coef_ref, res_ref, steps
+):
+    core = lax.rem(feat_ref[0], 2)
     fit = jnp.zeros((ROWS, TILE), F32)
     for b in range(BLOCKS):
         block = slice(b * BLK, (b + 1) * BLK)
         parts = []
-        gradient = rest_ref[b * 64 // 3 : b * 64 // 3 + 22, 16:40, :].reshape(22 * 24, TILE)
+        gradient = rest_ref[b * 64 // 3 : b * 64 // 3 + 22, 8:32, :].reshape(22 * 24, TILE)
         gradient = gradient[b * BLK - b * 64 // 3 * 24 :][:BLK] * (CLS / SAMPLES)
         for i in range(4):
             total = gradient[i * TILE : (i + 1) * TILE]
@@ -312,7 +337,9 @@
                 tiles = []
                 for j in range(4):
                     feat, slot = divmod(CROSS.index((b, a, i, j)), CROSS_SLOTS)
-                    tiles.append(cross_ref[feat, slot])
+                    place = (slot % 4, feat // 2, slice(None), slice(8 * (slot // 4), 8 * (slot // 4) + 8))
+                    tile = jnp.where(core == feat % 2, own_ref[place], other_ref[place])
+                    tiles.append(tile.reshape(TILE, TILE))
                 strip = jnp.concatenate(tiles, axis=1) * (1.0 / SAMPLES)
                 total = total - dot_exact(strip, steps[a * BLK : (a + 1) * BLK, :])
             parts.append(total)
@@ -322,7 +349,7 @@
             if i:
                 strip = jnp.concatenate([lower_ref[b, LOWER.index((i, j))] for j in range(i)], axis=1)
                 total = total + dot_exact(strip, jnp.concatenate(parts[:i], axis=0))
-            forward.append(dot_exact(pivot_ref[b, i], total))
+            forward.append(dot_exact(pivot_ref[b, i] if i < 3 else last_ref[b], total))
         for i in range(4):
             total = forward[i]
             if i < 3:
@@ -349,19 +376,19 @@
     res_ref[...] = (targets - fit / CLS)[:, :SHARE]
 
 
-def solve(feat, pivots, lower, cross, rest, features, labels):
+def solve(feat, pivots, last, lower, own, other, rest, features, labels):
     return pl.pallas_call(
         solve_kernel,
         out_shape=(
             jax.ShapeDtypeStruct((BLOCKS * BLK, SHARE), F32),
             jax.ShapeDtypeStruct((ROWS, SHARE), F32),
         ),
-        in_specs=[pl.BlockSpec(memory_space=pltpu.SMEM)] + full_specs(6),
+        in_specs=[pl.BlockSpec(memory_space=pltpu.SMEM)] + full_specs(8),
         out_specs=(pl.BlockSpec(memory_space=VMEM), pl.BlockSpec(memory_space=VMEM)),
         scratch_shapes=[VMEM((BLOCKS * BLK, TILE), F32)],
         compiler_params=pltpu.CompilerParams(vmem_limit_bytes=VMEM_LIMIT),
         name="solve",
-    )(feat, pivots, lower, cross, rest, features, labels)
+    )(feat, pivots, last, lower, own, other, rest, features, labels)
 
 
 def gather_by_exchange(value, axis, size):
@@ -389,17 +416,18 @@
     pieces = jnp.sum(lax.all_to_all(pieces, "z", 0, 0, tiled=True), axis=0)
     column = gather_by_exchange(pieces, "z", 16)
 
+    rest = lax.all_gather(column[:, 16:], "y", axis=0).reshape(64, 32, TILE)
     diag_own = gather_by_exchange(column[:, :8], ("y", "x"), 16).reshape(DIAG_SLOTS, 4, TILE, TILE)
     diag_other = swap_cores(diag_own)
-
-    rest = lax.all_gather(column[:, 8:], "y", axis=0)
-    rest, diag_own, diag_other = lax.optimization_barrier((rest, diag_own, diag_other))
-    rest = rest.reshape(64, 40, TILE)
-    cross = jnp.concatenate([rest[:, 0:8], rest[:32, 8:16]], axis=0).reshape(CROSS_SLOTS, TILE, TILE)
-    cross = lax.all_gather(cross, ("x", "c"), axis=0)
-
-    pivots, lower = factor(core1, diag_own, diag_other)
-    return solve(feat, pivots, lower, cross, rest, features, labels.reshape(1, ROWS))
+    crossing, diag_own = lax.optimization_barrier((column[:, 8:24], diag_own))
+    cross_own = gather_by_exchange(crossing, ("y", "x"), 16)
+
+    pivots, lower, last = factor(core1, diag_own, diag_other)
+    last, cross_own, rest = lax.optimization_barrier((last, cross_own, rest))
+    cross_own = cross_own.reshape(4, 4, 16, 16, TILE)
+    cross_other = swap_cores(cross_own)
+    last = last_pivots(last)
+    return solve(feat, pivots, last, lower, cross_own, cross_other, rest, features, labels.reshape(1, ROWS))
 
 
 def solution(mesh):

time: 232 us -> 234 us (level)
  the two profiles are of different devices: /device:TPU:1 before, /device:TPU:33 now
where the time goes in v3:
time: 234 us; the launch traced here: 230 us
  blocking collectives  119 us (51%)
  Pallas kernels  59.7 us (26%)
  starting transfers between devices  17.2 us (7%)
  between operations  14.3 us (6%)
  waiting for transfers between devices  13.8 us (6%)
  local copies, waits for them, and re-layouts  5.08 us (2%)
    all_to_all x2, blocking collectives, gather_by_exchange(): return lax.all_to_all(copies, axis, 0, 0, tiled=True)  47.5 us
    all_to_all x1, blocking collectives, per_device(): pieces = jnp.sum(lax.all_to_all(pieces, 'z', 0, 0, tiled=True), axis=0)  35.2 us
    pallas_call x1, Pallas kernels, factor(): pl.pallas_call(factor_kernel, out_shape=(jax.ShapeDtypeStruct((BLOCKS, 3,...  24.4 us
    all_to_all x1, blocking collectives, per_device(): lax.all_to_all(pieces.reshape(4, 16 * 48, TILE), 'y', 0, 0, tiled=True)  24 us
    ppermute x3, starting transfers between devices, swap_cores(): return lax.ppermute(value, 'c', [(0, 1), (1, 0)])  13 us
    pallas_call x1, Pallas kernels, local_features(): pl.pallas_call(conv_kernel, out_shape=jax.ShapeDtypeStruct((4 * LOCAL, RO...  12.5 us
    all_gather x1, blocking collectives, per_device(): own = lax.all_gather(panel, 'x', axis=0)  12.3 us
    pallas_call x1, Pallas kernels, solve(): pl.pallas_call(solve_kernel, out_shape=(jax.ShapeDtypeStruct((BLOCKS * BL...  12.1 us
  transfers between devices with their start and end apart: 5, of which 2 were waited for; matrix products, arithmetic and copies ran while one was open for 1% of the time, Pallas kernels for 14%

profile of v3, /device:TPU:33, one launch (start us, length us, event | category | flops | bytes accessed | tf_op | source)
XLA Modules:
  0.0 229.5 jit_solution(14716808425365288425)
XLA Ops:
  7.2 0.0 all-gather.4.cloned.1.call-start
  7.2 12.5 %features.1 = bf16[192,512]{1,0:T(8,128)(2,1)} custom-call(bf16[512,3072]{1,0:T(8,128)(2,1)} %x_ref.1, bf16[48,108]{1,0:T(8,128)(2,1)} %bitcast.25, bf16[108,768]{1,0:T(8,128)(2,1)} %constant.18.clone.place_ref, f32[3,16]{1,0:T(4,128)} %bias_ref.1), custom_call_target="tpu_custom_call" | custom-call | tf_op jit(solution)/shard_map/features/pallas_call | solution.py:122
  19.7 12.3 %all-gather = bf16[768,512]{1,0:T(8,128)(2,1)S(1)} all-gather(bf16[192,512]{1,0:T(8,128)(2,1)} %features.1), channel_id=2, replica_groups=mesh['y'=4,'z'=16,'x'=4,'c'=2] {'x'}, dimensions={0}, use_global_device_ids=true | all-gather | bytes 983040 | tf_op jit(solution)/shard_map/all_gather | solution.py:408
  32.0 4.1 %collective-permute-start = (bf16[4,192,512]{2,1,0:T(8,128)(2,1)S(1)}, bf16[4,192,512]{2,1,0:T(8,128)(2,1)S(1)}, u32[]{:S(2)}, u32[]{:S(2)}) collective-permute-start(bf16[4,192,512]{2,1,0:T(8,128)(2,1)S(1)} %bitcast.19), channel_id=1, source_target_pairs={{0,1},{1,0},{2,3},{3,2},{4,5},{5,4},{6,7},{7,6},{8,9},{9,8},{10,11... | collective-permute-start | bytes 2359304 | tf_op jit(solution)/shard_map/ppermute | solution.py:400
  36.1 1.9 collective-permute-done
  38.0 0.3 fusion
  38.3 1.3 copy.12
  39.6 3.5 %products.1 = f32[64,48,128]{2,1,0:T(8,128)} custom-call(s32[1]{0:T(128)} %bitcast.feat_ref, s32[8,20]{1,0:T(8,128)} %constant.19.clone.table_ref, bf16[1536,512]{1,0:T(8,128)(2,1)} %bitcast.14, s32[1,512]{1,0:T(1,128)} %bitcast.26), custom_call_target="tpu_custom_call" | custom-call | tf_op jit(solution)/shard_map/products/pallas_call | solution.py:160
  43.1 24.0 %all_to_all.25 = f32[4,768,128]{2,1,0:T(8,128)S(1)} all-to-all(f32[4,768,128]{2,1,0:T(8,128)} %bitcast.18), channel_id=1, replica_groups=mesh['y'=4,'z'=16,'x'=4,'c'=2] {'y'}, dimensions={0} | all-to-all | bytes 3145728 | tf_op jit(solution)/shard_map/all_to_all | solution.py:414
  67.1 0.1 reduce_sum.18
  67.2 35.2 %all_to_all.26 = f32[16,48,128]{2,1,0:T(8,128)S(1)} all-to-all(f32[16,48,128]{2,1,0:T(8,128)S(1)} %bitcast.21), channel_id=1, replica_groups=mesh['y'=4,'z'=16,'x'=4,'c'=2] {'z'}, dimensions={0} | all-to-all | bytes 786432 | tf_op jit(solution)/shard_map/all_to_all | solution.py:416
  102.5 28.8 %all_to_all.27 = f32[16,48,128]{2,1,0:T(8,128)S(1)} all-to-all(f32[16,48,128]{2,1,0:T(8,128)S(1)} %broadcast_in_dim.6), channel_id=1, replica_groups=mesh['y'=4,'z'=16,'x'=4,'c'=2] {'z'}, dimensions={0} | all-to-all | bytes 786432 | tf_op jit(solution)/shard_map/all_to_all | solution.py:396
  131.3 0.1 broadcast_in_dim.7
  131.4 18.7 %all_to_all.28 = f32[16,16,8,128]{3,2,1,0:T(8,128)S(1)} all-to-all(f32[16,16,8,128]{3,2,1,0:T(8,128)S(1)} %broadcast_in_dim.7), channel_id=1, replica_groups=mesh['y'=4,'z'=16,'x'=4,'c'=2] {'y','x'}, dimensions={0} | all-to-all | bytes 2097152 | tf_op jit(solution)/shard_map/all_to_all | solution.py:396
  150.1 0.0 copy-start.2
  150.1 6.1 %collective-permute-start.1 = (f32[4,4,128,128]{3,2,1,0:T(8,128)S(1)}, f32[4,4,128,128]{3,2,1,0:T(8,128)}, u32[]{:S(2)}, u32[]{:S(2)}) collective-permute-start(f32[4,4,128,128]{3,2,1,0:T(8,128)S(1)} %bitcast.22), channel_id=1, source_target_pairs={{0,1},{1,0},{2,3},{3,2},{4,5},{5,4},{6,7},{7,6},{8,9},{9,8},{10,11... | collective-permute-start | bytes 3145736 | tf_op jit(solution)/shard_map/ppermute | solution.py:400
  156.3 0.7 slice.14
  157.0 0.0 all-gather.4.cloned.1.call-update
  157.0 1.6 broadcast_in_dim.8
  158.6 0.0 copy-done.2
  158.6 4.2 %all-to-all-start.4 = ((f32[16,16,16,128]{3,2,1,0:T(8,128)}), f32[16,16,16,128]{3,2,1,0:T(8,128)S(1)}, u32[]{:S(2)}, u32[]{:S(2)}) async-start(f32[16,16,16,128]{3,2,1,0:T(8,128)} %broadcast_in_dim.8), calls=%async_computation.4 | async-start | bytes 4194304 | tf_op jit(solution)/shard_map/all_to_all | solution.py:396
  162.8 0.0 collective-permute-done.1.other_ref
  162.8 24.4 %factor.1 = (f32[3,3,128,128]{3,2,1,0:T(8,128)}, f32[3,6,128,128]{3,2,1,0:T(8,128)}, f32[3,16,8,128]{3,2,1,0:T(8,128)}) custom-call(s32[1]{0:T(128)} %bitcast.1.core_ref, f32[4,4,128,128]{3,2,1,0:T(8,128)} %bitcast.23, f32[4,4,128,128]{3,2,1,0:T(8,128)} %collective-permute-done.1.other_ref), custom_call_target="tpu_custom_call" | custom-call | flops 24999999488 | bytes 50000000 | tf_op jit(solution)/shard_map/factor/pallas_call | solution.py:308
  187.2 11.9 %all-gather.4.cloned.1.call-done.rest_ref = f32[64,32,128]{2,1,0:T(8,128)} async-done(((f32[16,32,128]{2,1,0:T(8,128)}), f32[64,32,128]{2,1,0:T(8,128)}) %all-gather.4.cloned.1.call-update) | async-done | bytes 1048592 | tf_op jit(solution)/shard_map/all_gather | solution.py:419
  199.1 0.0 all-to-all-done.4
  199.1 0.0 copy-start
  199.1 2.7 %collective-permute-start.2 = (f32[4,4,16,16,128]{4,3,2,1,0:T(8,128)S(1)}, f32[4,4,16,16,128]{4,3,2,1,0:T(8,128)S(1)}, u32[]{:S(2)}, u32[]{:S(2)}) collective-permute-start(f32[4,4,16,16,128]{4,3,2,1,0:T(8,128)S(1)} %bitcast.16), channel_id=1, source_target_pairs={{0,1},{1,0},{2,3},{3,2},{4,5},{5,4},{6,7},{7,6},{8,9},{9,8},{10,11... | collective-permute-start | bytes 6291464 | tf_op jit(solution)/shard_map/ppermute | solution.py:400
  201.8 7.2 %last_pivots.1.last_ref = f32[3,128,128]{2,1,0:T(8,128)} custom-call(f32[3,16,8,128]{3,2,1,0:T(8,128)} %get-tuple-element.14.last_ref), custom_call_target="tpu_custom_call" | custom-call | flops 5000000000 | bytes 10000000 | tf_op jit(solution)/shard_map/last_pivots/pallas_call | solution.py:295
  209.0 0.0 copy-done
  209.0 0.0 collective-permute-done.2.other_ref
  209.0 1.3 copy-done.1
  210.3 12.1 %solve.1 = (f32[1536,125]{1,0:T(8,128)}, f32[512,125]{1,0:T(8,128)}) custom-call(s32[1]{0:T(128)} %bitcast.feat_ref, f32[3,3,128,128]{3,2,1,0:T(8,128)} %get-tuple-element.11.pivot_ref, f32[3,128,128]{2,1,0:T(8,128)} %last_pivots.1.last_ref, f32[3,6,128,128]{3,2,1,0:T(8,128)} %get-tuple-element.15.lower_ref, f32[4,4,16,16,128]{4,3,2,1,0:T(8,128)} %bitcast.17, ...), custom_call_target="tpu_custom_call" | custom-call | tf_op jit(solution)/shard_map/solve/pallas_call | solution.py:380
  (5 shorter events, 0.1 us)
Async XLA Ops:
  7.2 191.9 %all-gather.4.cloned.1.call-start = ((), (), s32[]{:S(2)}) async-start(), calls=%async_computation.5 | async-start | bytes 1310720 | tf_op jit(solution)/shard_map/all_gather | solution.py:419
  32.0 6.0 %collective-permute-start = (bf16[4,192,512]{2,1,0:T(8,128)(2,1)S(1)}, bf16[4,192,512]{2,1,0:T(8,128)(2,1)S(1)}, u32[]{:S(2)}, u32[]{:S(2)}) collective-permute-start(bf16[4,192,512]{2,1,0:T(8,128)(2,1)S(1)} %bitcast.19), channel_id=1, source_target_pairs={{0,1},{1,0},{2,3},{3,2},{4,5},{5,4},{6,7},{7,6},{8,9},{9,8},{10,11... | collective-permute-start | bytes 2359304 | tf_op jit(solution)/shard_map/ppermute | solution.py:400
  150.1 8.5 %copy-start.2 = (f32[16,16,8,128]{3,2,1,0:T(8,128)}, f32[16,16,8,128]{3,2,1,0:T(8,128)S(1)}, u32[]{:S(2)}) copy-start(f32[16,16,8,128]{3,2,1,0:T(8,128)S(1)} %all_to_all.28) | copy-start | bytes 3145732
  150.1 12.7 %collective-permute-start.1 = (f32[4,4,128,128]{3,2,1,0:T(8,128)S(1)}, f32[4,4,128,128]{3,2,1,0:T(8,128)}, u32[]{:S(2)}, u32[]{:S(2)}) collective-permute-start(f32[4,4,128,128]{3,2,1,0:T(8,128)S(1)} %bitcast.22), channel_id=1, source_target_pairs={{0,1},{1,0},{2,3},{3,2},{4,5},{5,4},{6,7},{7,6},{8,9},{9,8},{10,11... | collective-permute-start | bytes 3145736 | tf_op jit(solution)/shard_map/ppermute | solution.py:400
  158.6 40.5 %all-to-all-start.4 = ((f32[16,16,16,128]{3,2,1,0:T(8,128)}), f32[16,16,16,128]{3,2,1,0:T(8,128)S(1)}, u32[]{:S(2)}, u32[]{:S(2)}) async-start(f32[16,16,16,128]{3,2,1,0:T(8,128)} %broadcast_in_dim.8), calls=%async_computation.4 | async-start | bytes 4194304 | tf_op jit(solution)/shard_map/all_to_all | solution.py:396
  199.1 9.9 %copy-start = (f32[16,16,16,128]{3,2,1,0:T(8,128)}, f32[16,16,16,128]{3,2,1,0:T(8,128)S(1)}, u32[]{:S(2)}) copy-start(f32[16,16,16,128]{3,2,1,0:T(8,128)S(1)} %all-to-all-done.4) | copy-start | bytes 6291460
  199.1 9.9 %collective-permute-start.2 = (f32[4,4,16,16,128]{4,3,2,1,0:T(8,128)S(1)}, f32[4,4,16,16,128]{4,3,2,1,0:T(8,128)S(1)}, u32[]{:S(2)}, u32[]{:S(2)}) collective-permute-start(f32[4,4,16,16,128]{4,3,2,1,0:T(8,128)S(1)} %bitcast.16), channel_id=1, source_target_pairs={{0,1},{1,0},{2,3},{3,2},{4,5},{5,4},{6,7},{7,6},{8,9},{9,8},{10,11... | collective-permute-start | bytes 6291464 | tf_op jit(solution)/shard_map/ppermute | solution.py:400
  209.0 1.3 copy-start.1
Sparse Core Ops, SparseCore 0:
  157.1 41.9 all-gather.3
